TPU v7x, 256 devices: a whole 4x4x8 slice. The times are simulated.
256 devices in a mesh: layer: 4 (over y), latent: 64 (over x, z, core).
Axes of the slice: x: 4, y: 4, z: 8, core: 2. Of those that a mesh axis runs over, the one named last changes fastest.
Arguments:
- acts: bfloat16 [4, 128, 3584], P('layer', 'latent'), may hold values from -6 to 6
- enc_weight: bfloat16 [4, 3584, 8192], P('layer', None, 'latent'), may hold values from -0.09375 to 0.09375
- enc_bias: float32 [4, 8192], P('layer', 'latent'), may hold values from -3 to 3
- active: int32 [4, 128, 8192], P('layer', None, 'latent'), may hold values 0 or 1
- dec_weight: bfloat16 [4, 4, 8192, 3584], P('layer', None, 'latent'), may hold values from -0.0625 to 0.0625
- dec_bias: float32 [4, 3584], replicated, may hold values from -3 to 3
- targets: bfloat16 [4, 128, 3584], P('layer', 'latent'), may hold values from -6 to 6
Outputs:
- grad_enc: bfloat16 [4, 3584, 8192], P('layer', None, 'latent')
- grad_enc_bias: float32 [4, 8192], P('layer', 'latent')
- grad_dec: bfloat16 [4, 4, 8192, 3584], P('layer', None, 'latent')
- grad_dec_bias: float32 [4, 3584], P('layer')
All inputs are finite; a program needn't handle non-finite values. No bound on the sum of `active` on one device may be relied on, other than what follows from the above.
Results may differ from a plain program's by a relative error of at most 0.0075.
Values may be sent and summed in bfloat16 or wider, within the bound.
No kernel may reach another device: no remote copies, remote signals or barrier semaphores. Data moves between devices by JAX's collectives and lax.ppermute only.
A program may use at most 128 MiB of HBM per device.

v0:
```python
import jax
import jax.numpy as jnp
from jax import lax
from jax.sharding import PartitionSpec as P


def per_device(acts, enc_weight, enc_bias, active, dec_weight, dec_bias, targets):
    layers = dec_weight.shape[1]
    width = acts.shape[2]
    source = lax.axis_index("layer")
    whole = lax.all_gather(acts, "latent", axis=1, tiled=True)[0]
    rows = whole.shape[0]
    pre = jnp.dot(whole, enc_weight[0], preferred_element_type=jnp.float32) + enc_bias[0][None, :]
    gate = active[0].astype(jnp.float32)
    feats = (pre * gate).astype(jnp.bfloat16)
    keep = (jnp.arange(layers) >= source).astype(jnp.float32)
    decoder = dec_weight[0]
    partial_sums = (
        jnp.einsum("bf,tfd->tbd", feats, decoder, preferred_element_type=jnp.float32)
        * keep[:, None, None]
    )
    summed = lax.psum_scatter(
        partial_sums.reshape(layers * rows, width),
        ("layer", "latent"),
        scatter_dimension=0,
        tiled=True,
    )
    bias_row = lax.dynamic_index_in_dim(dec_bias, source, 0, keepdims=False)
    scale = rows ** (-0.5)
    err = ((summed + bias_row[None, :] - targets[0].astype(jnp.float32)) * scale).astype(
        jnp.bfloat16
    )
    err_all = lax.all_gather(err, ("layer", "latent"), axis=0, tiled=True).reshape(
        layers, rows, width
    )
    err_kept = err_all * keep.astype(jnp.bfloat16)[:, None, None]
    back = jnp.einsum("tbd,tfd->bf", err_kept, decoder, preferred_element_type=jnp.float32)
    grads = jnp.einsum("bf,tbd->tfd", feats, err_kept, preferred_element_type=jnp.float32).astype(
        jnp.bfloat16
    )
    dpre = (back * gate).astype(jnp.bfloat16)
    grad_enc = lax.dot_general(
        whole, dpre, (((0,), (0,)), ((), ())), preferred_element_type=jnp.float32
    ).astype(jnp.bfloat16)
    grad_enc_bias = jnp.sum(dpre.astype(jnp.float32), axis=0)
    grad_dec_bias = jnp.sum(err_all.astype(jnp.float32), axis=1)
    own_bias = lax.dynamic_index_in_dim(grad_dec_bias, source, 0, keepdims=True)
    return (grad_enc[None], grad_enc_bias[None], grads[None], own_bias)


def solution(mesh):
    return jax.shard_map(
        per_device,
        mesh=mesh,
        in_specs=(
            P("layer", "latent", None),
            P("layer", None, "latent"),
            P("layer", "latent"),
            P("layer", None, "latent"),
            P("layer", None, "latent", None),
            P(),
            P("layer", "latent", None),
        ),
        out_specs=(
            P("layer", None, "latent"),
            P("layer", "latent"),
            P("layer", None, "latent", None),
            P("layer", None),
        ),
        check_vma=False,
    )
```

profile of v0, /device:TPU:1, one launch (start us, length us, event | category | flops | bytes accessed | tf_op | source)
XLA Modules:
  0.0 501.3 jit_solution(1748207111064871138)
XLA Ops:
  7.2 0.0 copy-start
  7.2 0.0 all-reduce.3.cloned.1.call-start
  7.2 0.0 copy-start.2
  7.3 0.9 copy.20
  8.1 55.4 %all_gather.6 = bf16[1,128,3584]{2,0,1:T(2,128)(2,1)S(1)} all-gather(bf16[1,2,3584]{2,0,1:T(2,128)(2,1)S(1)} %copy.20), channel_id=1, replica_groups=mesh['layer'=4,'latent'=64] {'latent'}, dimensions={1}, use_global_device_ids=true | all-gather | bytes 931840 | tf_op jit(solution)/shard_map/all_gather | solution.py:11
  63.5 0.0 copy-done
  63.6 1.2 fusion.26
  64.8 0.0 copy-done.2
  64.8 4.1 convolution_multiply_fusion
  68.9 0.0 copy-start.4
  68.9 0.0 all-reduce.3.cloned.1.call-update
  68.9 0.0 all-gather.3.cloned.1.call-start
  69.0 0.9 dynamic-slice_reduce_fusion
  69.9 271.2 %all-reduce.3.cloned.1.call-done = f32[512,3584]{1,0:T(8,128)} async-done(((f32[512,3584]{1,0:T(8,128)}), f32[512,3584]{1,0:T(8,128)}) %all-reduce.3.cloned.1.call-update) | async-done | bytes 7340048
  341.1 0.0 copy-done.4
  341.1 1.5 fusion.34
  342.6 0.0 all-gather.3.cloned.1.call-update
  342.7 117.7 %all-gather.3.cloned.1.call-done = bf16[256,2,3584]{2,1,0:T(2,128)(2,1)} async-done(((bf16[1,2,3584]{2,1,0:T(2,128)(2,1)}), bf16[256,2,3584]{2,1,0:T(2,128)(2,1)}) %all-gather.3.cloned.1.call-update) | async-done | bytes 3670032 | tf_op jit(solution)/shard_map/all_gather | solution.py:33
  460.4 8.4 %reshape.26 = bf16[4,128,3584]{2,1,0:T(8,128)(2,1)} reshape(bf16[256,2,3584]{2,1,0:T(2,128)(2,1)} %all-gather.3.cloned.1.call-done) | data formatting | bytes 7340032 | tf_op jit(solution)/shard_map/reshape | solution.py:33
  468.8 2.6 convert_reduce_fusion
  471.4 0.0 copy-start.5
  471.4 6.0 %copy.21 = bf16[4,128,3584]{1,2,0:T(8,128)(2,1)} copy(bf16[4,128,3584]{2,1,0:T(8,128)(2,1)} %reshape.26) | data formatting | bytes 7340032 | tf_op jit(solution)/shard_map/reshape | solution.py:33
  477.4 0.0 copy-start.1
  477.4 0.0 copy-start.3
  477.4 5.2 %fusion = bf16[1,4,128,3584]{2,3,1,0:T(8,128)(2,1)} fusion(bf16[128,128,1]{1,0,2:T(8,128)(2,1)S(1)} %fusion.26, bf16[4,128,3584]{1,2,0:T(8,128)(2,1)} %copy.21, bf16[4]{0:T(256)(128)(2,1)S(1)} %fusion.35), kind=kOutput, calls=%fused_computation.3 | convolution fusion | flops 473432064 | bytes 7372808 | tf_op jit(solution)/shard_map/bf,tbd->tfd/dot_general | solution.py:38
  482.6 0.0 copy-done.5
  482.6 0.0 copy-done.1
  482.6 0.0 copy-done.3
  482.6 1.8 convert_reduce_fusion.1
  484.4 0.6 constant_dynamic-slice_fusion
  485.0 5.9 %copy.24 = bf16[1,4,128,3584]{3,2,1,0:T(8,128)(2,1)} copy(bf16[1,4,128,3584]{2,3,1,0:T(8,128)(2,1)} %fusion) | data formatting | bytes 7340032
  490.9 1.3 fusion.1
  492.3 2.2 copy.23
  (2 shorter events, 0.0 us)
Async XLA Ops:
  7.2 56.4 %copy-start = (bf16[1,3584,128]{2,1,0:T(8,128)(2,1)S(1)}, bf16[1,3584,128]{2,1,0:T(8,128)(2,1)}, u32[]{:S(2)}) copy-start(bf16[1,3584,128]{2,1,0:T(8,128)(2,1)} %param.8) | copy-start | bytes 2752516
  7.2 333.9 %all-reduce.3.cloned.1.call-start = ((), (), s32[]{:S(2)}) async-start(), calls=%async_computation.1 | async-start | bytes 14680064
  7.2 57.6 %copy-start.2 = (bf16[1,4,128,3584]{3,2,1,0:T(8,128)(2,1)S(1)}, bf16[1,4,128,3584]{3,2,1,0:T(8,128)(2,1)}, u32[]{:S(2)}) copy-start(bf16[1,4,128,3584]{3,2,1,0:T(8,128)(2,1)} %param.11) | copy-start | bytes 11010052
  68.9 272.2 %copy-start.4 = (bf16[1,2,3584]{2,1,0:T(2,128)(2,1)S(1)}, bf16[1,2,3584]{2,1,0:T(2,128)(2,1)}, u32[]{:S(2)}) copy-start(bf16[1,2,3584]{2,1,0:T(2,128)(2,1)} %param.13) | copy-start | bytes 43012
  68.9 391.5 %all-gather.3.cloned.1.call-start = ((), (), s32[]{:S(2)}) async-start(), calls=%async_computation | async-start | bytes 3684352 | tf_op jit(solution)/shard_map/all_gather | solution.py:33
  471.4 11.2 %copy-start.5 = (s32[1,128,128]{2,1,0:T(8,128)S(1)}, s32[1,128,128]{2,1,0:T(8,128)}, u32[]{:S(2)}) copy-start(s32[1,128,128]{2,1,0:T(8,128)} %param.10) | copy-start | bytes 196612
  477.4 5.2 %copy-start.1 = (bf16[4,128,3584]{1,2,0:T(8,128)(2,1)S(1)}, bf16[4,128,3584]{1,2,0:T(8,128)(2,1)}, u32[]{:S(2)}) copy-start(bf16[4,128,3584]{1,2,0:T(8,128)(2,1)} %copy.21) | copy-start | bytes 11010052
  477.4 5.2 %copy-start.3 = (bf16[1,4,128,3584]{3,2,1,0:T(8,128)(2,1)S(1)}, bf16[1,4,128,3584]{3,2,1,0:T(8,128)(2,1)}, u32[]{:S(2)}) copy-start(bf16[1,4,128,3584]{3,2,1,0:T(8,128)(2,1)} %param.11) | copy-start | bytes 11010052
Sparse Core Ops, SparseCore 0:
  69.1 272.0 all-reduce.2
  345.5 114.9 all-gather.2
where the time goes:
time: 502 us; the launch traced here: 501 us
  waiting for transfers between devices  389 us (77%)
  blocking collectives  55.4 us (11%)
  local copies, waits for them, and re-layouts  24.9 us (5%)
  between operations  14.1 us (3%)
  matrix products  13.6 us (3%)
    unnamed x3, waiting for transfers between devices  271 us
    all_gather x1, waiting for transfers between devices, per_device(): lax.all_gather(err, ('layer', 'latent'), axis=0, tiled=True)  118 us
    all_gather x1, blocking collectives, per_device(): whole = lax.all_gather(acts, 'latent', axis=1, tiled=True)[0]  55.4 us
    reshape x2, local copies, waits for them, and re-layouts, per_device(): lax.all_gather(err, ('layer', 'latent'), axis=0, tiled=True)  14.4 us
  transfers between devices with their start and end apart: 2, of which 2 were waited for; matrix products, arithmetic and copies ran while one was open for 0% of the time, Pallas kernels for 0%

commit v1 on v0

v1 whole, which is shorter than its diff:
```python
import jax
import jax.numpy as jnp
from jax import lax
from jax.experimental import pallas as pl
from jax.experimental.pallas import tpu as pltpu
from jax.sharding import Mesh
from jax.sharding import PartitionSpec as P

LAYERS = 4
SWAP = [(0, 1), (1, 0)]
BF16 = jnp.bfloat16
F32 = jnp.float32


def ring(shift):
    return [(i, (i + shift) % LAYERS) for i in range(LAYERS)]


def grads_kernel(places, feats_t, own, other, decoder, back_in, *refs):
    grad_ref, back_ref = refs[-2:]
    step = pl.program_id(0)

    @pl.when(step == 0)
    def _():
        back_ref[...] = back_in[...]

    @pl.when(places[2] == 0)
    def _():
        grad_ref[...] = jnp.zeros_like(grad_ref)

    def work(block):
        tile = block[:, 0].reshape(feats_t.shape[1], block.shape[3])
        grad_ref[0] = jnp.dot(feats_t[...], tile, preferred_element_type=F32).astype(BF16)
        back_ref[...] += lax.dot_general(
            tile, decoder[0], (((1,), (1,)), ((), ())), preferred_element_type=F32
        )

    @pl.when((places[2] == 1) & (step < 2))
    def _():
        work(own)

    @pl.when((places[2] == 1) & (step >= 2))
    def _():
        work(other)


def grads_of_target(places, feats_t, own, other, decoder, back, grads):
    layers, latents, width = decoder.shape
    rows = feats_t.shape[1]
    quarter = width // 4

    def lanes(step, places):
        half = jnp.where(step < 2, places[1], 1 - places[1])
        return 2 * half + step % 2

    whole = lambda step, places: (0, 0)
    wide = lambda step, places: (places[0], 0, lanes(step, places))
    in_specs = [
        pl.BlockSpec((latents, rows), whole),
        pl.BlockSpec((rows // 8, 1, 8, quarter), lambda step, places: (0, jnp.minimum(step, 1), 0, 0)),
        pl.BlockSpec((rows // 8, 1, 8, quarter), lambda step, places: (0, jnp.maximum(step - 2, 0), 0, 0)),
        pl.BlockSpec((1, latents, quarter), wide),
        pl.BlockSpec((rows, latents), whole),
    ]
    operands = [places, feats_t, own, other, decoder, back]
    aliases = {}
    if grads is not None:
        in_specs.append(pl.BlockSpec(memory_space=pl.ANY))
        operands.append(grads)
        aliases = {6: 0}
    return pl.pallas_call(
        grads_kernel,
        grid_spec=pltpu.PrefetchScalarGridSpec(
            num_scalar_prefetch=1,
            grid=(4,),
            in_specs=in_specs,
            out_specs=[pl.BlockSpec((1, latents, quarter), wide), pl.BlockSpec((rows, latents), whole)],
        ),
        out_shape=[
            jax.ShapeDtypeStruct(decoder.shape, BF16),
            jax.ShapeDtypeStruct((rows, latents), F32),
        ],
        input_output_aliases=aliases,
        compiler_params=pltpu.CompilerParams(vmem_limit_bytes=32 * 1024 * 1024),
        cost_estimate=pl.CostEstimate(
            flops=4 * rows * latents * width, bytes_accessed=6 * latents * width, transcendentals=0
        ),
        name="grads_of_target",
    )(*operands)


def encoder_kernel(acts, back, gate, grad_ref, bias_ref):
    dpre = (back[...] * gate[...].astype(F32)).astype(BF16)
    grad_ref[...] = lax.dot_general(
        acts[...], dpre, (((0,), (0,)), ((), ())), preferred_element_type=F32
    ).astype(BF16)
    bias_ref[...] = jnp.sum(dpre.astype(F32), axis=0, keepdims=True)


def encoder_grads(acts, back, active):
    rows, width = acts.shape
    latents = back.shape[1]
    block = width // 7
    whole = lambda step: (0, 0)
    return pl.pallas_call(
        encoder_kernel,
        grid=(7,),
        in_specs=[
            pl.BlockSpec((rows, block), lambda step: (0, step)),
            pl.BlockSpec((rows, latents), whole),
            pl.BlockSpec((rows, latents), whole),
        ],
        out_specs=[pl.BlockSpec((block, latents), lambda step: (step, 0)), pl.BlockSpec((1, latents), whole)],
        out_shape=[jax.ShapeDtypeStruct((width, latents), BF16), jax.ShapeDtypeStruct((1, latents), F32)],
        compiler_params=pltpu.CompilerParams(vmem_limit_bytes=32 * 1024 * 1024),
        cost_estimate=pl.CostEstimate(
            flops=2 * rows * latents * width, bytes_accessed=4 * latents * width, transcendentals=0
        ),
        name="encoder_grads",
    )(acts, back, active)


def per_device(acts, enc_weight, enc_bias, active, dec_weight, dec_bias, targets):
    layer, core = lax.axis_index("y"), lax.axis_index("c")
    chip = lax.axis_index(("x", "z"))
    decoder = dec_weight[0]
    layers, latents, width = decoder.shape
    half, quarter = width // 2, width // 4
    rows = active.shape[1]
    scale = rows ** (-0.5)

    mine = lax.dynamic_slice_in_dim(decoder, core * half, half, axis=2)
    give = lax.dynamic_slice_in_dim(decoder, (1 - core) * half, half, axis=2)
    got = lax.ppermute(give, "c", SWAP)
    target_mine = lax.dynamic_slice_in_dim(targets[0], core * half, half, axis=1)
    target_give = lax.dynamic_slice_in_dim(targets[0], (1 - core) * half, half, axis=1)
    target_got = lax.ppermute(target_give, "c", SWAP)
    target_rows = jnp.where(
        core == 0,
        jnp.concatenate([target_mine, target_got], axis=0),
        jnp.concatenate([target_got, target_mine], axis=0),
    ).astype(F32)

    devices = rows // acts.shape[1]
    copies = jnp.broadcast_to(acts[0][None], (devices,) + acts.shape[1:])
    whole = lax.all_to_all(copies, ("x", "z", "c"), 0, 0, tiled=True).reshape(rows, width)
    pre = jnp.dot(whole, enc_weight[0], preferred_element_type=F32) + enc_bias[0][None, :]
    gate = active[0].astype(F32)
    feats = (pre * gate).astype(BF16)
    feats_other = lax.ppermute(feats, "c", SWAP)

    def partial(shift):
        target = (layer + shift) % layers
        first = lax.dynamic_index_in_dim(mine, target, 0, keepdims=False)
        second = lax.dynamic_index_in_dim(got, target, 0, keepdims=False)
        return jnp.dot(feats, first, preferred_element_type=F32) + jnp.dot(
            feats_other, second, preferred_element_type=F32
        )

    arrived = []
    for shift in (3, 2, 1):
        arrived.append(lax.ppermute(partial(shift).astype(BF16), "y", ring(shift)))
    total = partial(0)
    placed = lax.dynamic_update_slice_in_dim(
        jnp.zeros((rows, half), F32), target_rows, chip * target_rows.shape[0], 0
    )
    total = total - placed
    for shift, block in zip((3, 2, 1), arrived):
        total = total + jnp.where(layer >= shift, block.astype(F32), 0.0)
    chunks = (
        total.astype(BF16).reshape(rows // 8, 8, 2, quarter).transpose(0, 2, 1, 3).reshape(-1, 8, quarter)
    )
    pieces = lax.all_to_all(chunks, ("x", "z"), 0, 0, tiled=True)
    summed = jnp.sum(pieces.astype(F32), axis=0)
    bias = lax.dynamic_slice(dec_bias, (layer, core * half + (chip % 2) * quarter), (1, quarter))
    err = ((summed + bias) * scale).astype(BF16)
    err_copies = jnp.broadcast_to(err[None], (rows // 4, 8, quarter))
    own = lax.all_to_all(err_copies, ("x", "z"), 0, 0, tiled=True).reshape(rows // 8, 2, 8, quarter)

    errs = [own] + [lax.ppermute(own, "y", ring(-shift)) for shift in (1, 2, 3)]
    feats_t = feats.T
    back = jnp.zeros((rows, latents), F32)
    grads = None
    for shift, mine_err in enumerate(errs):
        other_err = lax.ppermute(mine_err, "c", SWAP)
        if shift == 0:
            sums = jnp.stack(
                [jnp.sum(e.astype(F32), axis=(0, 2)).reshape(half) for e in (mine_err, other_err)]
            )
            sums = jnp.where(core == 0, sums, sums[::-1]).reshape(1, width)
        places = jnp.stack(
            [(layer + shift) % layers, core, (layer + shift < layers).astype(jnp.int32)]
        ).astype(jnp.int32)
        grads, back = grads_of_target(places, feats_t, mine_err, other_err, decoder, back, grads)
    grad_enc, grad_enc_bias = encoder_grads(whole, back, active[0])
    return grad_enc[None], grad_enc_bias, grads[None], sums


def solution(mesh):
    split = Mesh(mesh.devices.reshape(4, 4, 8, 2), ("y", "x", "z", "c"))
    latent = ("x", "z", "c")
    return jax.shard_map(
        per_device,
        mesh=split,
        in_specs=(
            P("y", latent, None),
            P("y", None, latent),
            P("y", latent),
            P("y", None, latent),
            P("y", None, latent, None),
            P(),
            P("y", latent, None),
        ),
        out_specs=(
            P("y", None, latent),
            P("y", latent),
            P("y", None, latent, None),
            P("y", None),
        ),
        check_vma=False,
    )
```

time: 502 us -> 168 us (0.33)
  waiting for transfers between devices: 389 us -> 85.8 us
  blocking collectives: 55.4 us -> 0 us
  starting transfers between devices: 0.08 us -> 39.8 us
  Pallas kernels: 0 us -> 17.7 us
  local copies, waits for them, and re-layouts: 24.9 us -> 10.3 us
  between operations: 14.1 us -> 0.96 us
    unnamed x3 -> x0, waiting for transfers between devices: 271 us -> none
    all_gather x1 -> x0, waiting for transfers between devices: 118 us -> none  [per_device(): lax.all_gather(err, ('layer', 'latent'), axis=0, tiled=True)]
    all_gather x1 -> x0, blocking collectives: 55.4 us -> none  [per_device(): whole = lax.all_gather(acts, 'latent', axis=1, tiled=True)[0]]
    all_to_all x0 -> x3, waiting for transfers between devices: none -> 46.8 us  [the longest x1 22.2 us: per_device(): lax.all_to_all(copies, ('x', 'z', 'c'), 0, 0, tiled=True)]
    ppermute x0 -> x13, waiting for transfers between devices: none -> 39 us  [the longest x3 19.8 us: per_device(): arrived.append(lax.ppermute(partial(shift).astype(BF16), 'y', ring(shift)))]
    all_to_all x0 -> x3, starting transfers between devices: none -> 26.1 us  [the longest x1 13.1 us: per_device(): lax.all_to_all(copies, ('x', 'z', 'c'), 0, 0, tiled=True)]
    pallas_call x0 -> x5, Pallas kernels: none -> 17.7 us  [the longest x4 14.1 us: grads_of_target(): pl.pallas_call(grads_kernel, grid_spec=pltpu.PrefetchScalarGridSpec(num_s...]
    reshape x2 -> x1, local copies, waits for them, and re-layouts: 14.4 us -> 0.34 us  [per_device(): lax.all_to_all(copies, ('x', 'z', 'c'), 0, 0, tiled=True)]
  transfers between devices with their start and end apart: 2 -> 16, of which waited for: 2 -> 8; matrix products, arithmetic and copies ran while one was open for 0% -> 10% of each run, Pallas kernels for 0% -> 7%
where the time goes in v1:
time: 168 us
  waiting for transfers between devices  85.8 us (51%)
  starting transfers between devices  39.8 us (24%)
  Pallas kernels  17.7 us (11%)
  matrix products  12.1 us (7%)
  local copies, waits for them, and re-layouts  10.3 us (6%)
    all_to_all x1, waiting for transfers between devices, per_device(): lax.all_to_all(copies, ('x', 'z', 'c'), 0, 0, tiled=True)  22.2 us
    ppermute x3, waiting for transfers between devices, per_device(): arrived.append(lax.ppermute(partial(shift).astype(BF16), 'y', ring(shift)))  19.8 us
    ppermute x3, waiting for transfers between devices, per_device(): errs = [own] + [lax.ppermute(own, 'y', ring(-shift)) for shift in (1, 2, 3)]  19.1 us
    pallas_call x4, Pallas kernels, grads_of_target(): pl.pallas_call(grads_kernel, grid_spec=pltpu.PrefetchScalarGridSpec(num_s...  14.1 us
    all_to_all x1, starting transfers between devices, per_device(): lax.all_to_all(copies, ('x', 'z', 'c'), 0, 0, tiled=True)  13.1 us
    all_to_all x1, waiting for transfers between devices, per_device(): pieces = lax.all_to_all(chunks, ('x', 'z'), 0, 0, tiled=True)  12.3 us
    all_to_all x1, waiting for transfers between devices, per_device(): lax.all_to_all(err_copies, ('x', 'z'), 0, 0, tiled=True)  12.2 us
    all_to_all x1, starting transfers between devices, per_device(): lax.all_to_all(err_copies, ('x', 'z'), 0, 0, tiled=True)  7.58 us
  transfers between devices with their start and end apart: 16, of which 8 were waited for; matrix products, arithmetic and copies ran while one was open for 10% of the time, Pallas kernels for 7%

profile of v1, /device:TPU:1, one launch (start us, length us, event | category | flops | bytes accessed | tf_op | source)
XLA Modules:
  0.0 167.5 jit_solution(12621320030297807799)
XLA Ops:
  0.7 2.2 %broadcast_in_dim.30 = bf16[64,2,3584]{2,1,0:T(2,128)(2,1)} broadcast(bf16[2,3584]{1,0:T(2,128)(2,1)} %bitcast.93), dimensions={1,2} | broadcast | bytes 931840 | tf_op jit(solution)/shard_map/broadcast_in_dim | solution.py:145
  2.9 13.1 %all-to-all-start = ((bf16[64,2,3584]{2,1,0:T(2,128)(2,1)}), bf16[64,2,3584]{2,1,0:T(2,128)(2,1)S(1)}, u32[]{:S(2)}, u32[]{:S(2)}) async-start(bf16[64,2,3584]{2,1,0:T(2,128)(2,1)} %broadcast_in_dim.30), calls=%async_computation | async-start | bytes 1835008 | tf_op jit(solution)/shard_map/all_to_all | solution.py:146
  16.0 2.9 %dynamic-slice_bitcast_fusion = bf16[4,128,1792]{2,1,0:T(8,128)(2,1)} fusion(bf16[1,4,128,3584]{3,2,1,0:T(8,128)(2,1)} %param.11, s32[]{:T(128)S(6)} %select_n.117), kind=kLoop, calls=%fused_computation.12 | loop fusion | bytes 3670020 | tf_op jit(solution)/shard_map/dynamic_slice | solution.py:133
  18.8 0.5 collective-permute-start.1
  19.3 0.1 collective-permute-start.2
  19.5 22.2 %all-to-all-done = bf16[64,2,3584]{2,1,0:T(2,128)(2,1)S(1)} async-done(((bf16[64,2,3584]{2,1,0:T(2,128)(2,1)}), bf16[64,2,3584]{2,1,0:T(2,128)(2,1)S(1)}, u32[]{:S(2)}, u32[]{:S(2)}) %all-to-all-start) | async-done | bytes 917536 | tf_op jit(solution)/shard_map/all_to_all | solution.py:146
  41.7 0.3 reshape.57.acts
  42.1 0.4 fusion.9
  42.5 0.4 collective-permute-start
  42.9 1.4 fusion.18
  44.3 1.4 fusion.15
  45.7 1.4 fusion.12
  47.2 1.3 fusion.5
  48.5 2.8 %collective-permute-start.3 = (bf16[128,1792]{1,0:T(8,128)(2,1)S(1)}, bf16[128,1792]{1,0:T(8,128)(2,1)S(1)}, u32[]{:S(2)}, u32[]{:S(2)}) collective-permute-start(bf16[128,1792]{1,0:T(8,128)(2,1)S(1)} %fusion.5), channel_id=1, source_target_pairs={{0,192},{64,0},{128,64},{192,128},{1,193},{65,1},{129,65},{193,129... | collective-permute-start | bytes 1376264 | tf_op jit(solution)/shard_map/ppermute | solution.py:162
  51.3 1.3 fusion.6
  52.6 0.4 collective-permute-start.4
  53.0 1.3 fusion.7
  54.3 0.8 collective-permute-start.5
  55.2 1.4 fusion.21
  56.6 14.1 %collective-permute-done.3 = bf16[128,1792]{1,0:T(8,128)(2,1)S(1)} collective-permute-done((bf16[128,1792]{1,0:T(8,128)(2,1)S(1)}, bf16[128,1792]{1,0:T(8,128)(2,1)S(1)}, u32[]{:S(2)}, u32[]{:S(2)}) %collective-permute-start.3) | collective-permute-done | bytes 458784 | tf_op jit(solution)/shard_map/ppermute | solution.py:162
  70.7 5.8 %collective-permute-done.5 = bf16[128,1792]{1,0:T(8,128)(2,1)S(1)} collective-permute-done((bf16[128,1792]{1,0:T(8,128)(2,1)S(1)}, bf16[128,1792]{1,0:T(8,128)(2,1)S(1)}, u32[]{:S(2)}, u32[]{:S(2)}) %collective-permute-start.5) | collective-permute-done | bytes 458784 | tf_op jit(solution)/shard_map/ppermute | solution.py:162
  76.4 2.2 %fusion.4 = bf16[128,1792]{1,0:T(8,128)(2,1)} fusion(f32[128,1792]{1,0:T(8,128)S(1)} %convert_dynamic-update-slice_fusion, f32[128,1792]{1,0:T(8,128)S(1)} %fusion.21, bf16[128,128]{1,0:T(8,128)(2,1)S(1)} %collective-permute-done, bf16[128,1792]{1,0:T(8,128)(2,1)S(1)} %collective-permute-done.5, bf16[128,1792]{1,0:T(8,128)(2,1)S(1)} %collective-permute-done.4, ...), kind=kOutput, calls=%fused_computation.8 | convolution fusion | flops 61472768 | bytes 4161543 | tf_op jit(solution)/shard_map/dot_general | solution.py:156
  78.7 5.4 %all-to-all-start.1 = ((bf16[32,8,896]{2,1,0:T(8,128)(2,1)}), bf16[32,8,896]{2,1,0:T(8,128)(2,1)S(1)}, u32[]{:S(2)}, u32[]{:S(2)}) async-start(bf16[32,8,896]{2,1,0:T(8,128)(2,1)} %bitcast.21), calls=%async_computation.1 | async-start | bytes 917504 | tf_op jit(solution)/shard_map/all_to_all | solution.py:173
  84.1 0.8 dynamic-slice_reduce_fusion
  84.9 12.3 %all-to-all-done.1 = bf16[32,8,896]{2,1,0:T(8,128)(2,1)S(1)} async-done(((bf16[32,8,896]{2,1,0:T(8,128)(2,1)}), bf16[32,8,896]{2,1,0:T(8,128)(2,1)S(1)}, u32[]{:S(2)}, u32[]{:S(2)}) %all-to-all-start.1) | async-done | bytes 458784 | tf_op jit(solution)/shard_map/all_to_all | solution.py:173
  97.3 0.8 broadcast_in_dim.32
  98.1 7.6 %all-to-all-start.2 = ((bf16[32,8,896]{2,1,0:T(8,128)(2,1)}), bf16[32,8,896]{2,1,0:T(8,128)(2,1)S(1)}, u32[]{:S(2)}, u32[]{:S(2)}) async-start(bf16[32,8,896]{2,1,0:T(8,128)(2,1)} %broadcast_in_dim.32), calls=%async_computation.2 | async-start | bytes 917504 | tf_op jit(solution)/shard_map/all_to_all | solution.py:178
  105.8 12.2 %all-to-all-done.2 = bf16[32,8,896]{2,1,0:T(8,128)(2,1)S(1)} async-done(((bf16[32,8,896]{2,1,0:T(8,128)(2,1)}), bf16[32,8,896]{2,1,0:T(8,128)(2,1)S(1)}, u32[]{:S(2)}, u32[]{:S(2)}) %all-to-all-start.2) | async-done | bytes 458784 | tf_op jit(solution)/shard_map/all_to_all | solution.py:178
  118.1 4.3 %collective-permute-start.12 = (bf16[16,2,8,896]{3,2,1,0:T(8,128)(2,1)S(1)}, bf16[16,2,8,896]{3,2,1,0:T(8,128)(2,1)S(1)}, u32[]{:S(2)}, u32[]{:S(2)}) collective-permute-start(bf16[16,2,8,896]{3,2,1,0:T(8,128)(2,1)S(1)} %bitcast.79), channel_id=1, source_target_pairs={{0,1},{1,0},{2,3},{3,2},{4,5},{5,4},{6,7},{7,6},{8,9},{9,8},{10,11... | collective-permute-start | bytes 1376264 | tf_op jit(solution)/shard_map/ppermute | solution.py:185
  122.6 0.1 copy.25.feats_t
  122.8 0.4 collective-permute-start.8
  123.2 1.0 collective-permute-start.6
  124.2 0.3 convert_reduce_fusion.1
  124.7 0.1 convert_reduce_fusion
  124.8 0.4 rev.3
  125.2 9.8 %collective-permute-done.10.own = bf16[16,2,8,896]{3,2,1,0:T(8,128)(2,1)} collective-permute-done((bf16[16,2,8,896]{3,2,1,0:T(8,128)(2,1)S(1)}, bf16[16,2,8,896]{3,2,1,0:T(8,128)(2,1)}, u32[]{:S(2)}, u32[]{:S(2)}) %collective-permute-start.10) | collective-permute-done | bytes 458784 | tf_op jit(solution)/shard_map/ppermute | solution.py:180
  135.0 1.2 collective-permute-start.11
  136.2 0.5 collective-permute-done.8.own
  136.7 1.2 collective-permute-start.9
  137.8 8.8 %collective-permute-done.6.own = bf16[16,2,8,896]{3,2,1,0:T(8,128)(2,1)S(1)} collective-permute-done((bf16[16,2,8,896]{3,2,1,0:T(8,128)(2,1)S(1)}, bf16[16,2,8,896]{3,2,1,0:T(8,128)(2,1)S(1)}, u32[]{:S(2)}, u32[]{:S(2)}) %collective-permute-start.6) | collective-permute-done | bytes 458784 | tf_op jit(solution)/shard_map/ppermute | solution.py:180
  146.7 0.5 collective-permute-start.7
  147.2 0.6 copy.30
  147.8 2.0 %copy-done.1 = bf16[1,4,128,3584]{3,2,1,0:T(8,128)(2,1)S(1)} copy-done((bf16[1,4,128,3584]{3,2,1,0:T(8,128)(2,1)S(1)}, bf16[1,4,128,3584]{3,2,1,0:T(8,128)(2,1)}, u32[]{:S(2)}) %copy-start.1) | copy-done | bytes 3670040
  149.8 3.2 %grads_of_target.4 = (bf16[4,128,3584]{2,1,0:T(8,128)(2,1)}, f32[128,128]{1,0:T(8,128)S(1)}) custom-call(s32[3]{0:T(128)S(1)} %pad_add_fusion.3.places, bf16[128,128]{1,0:T(8,128)(2,1)S(1)} %copy.25.feats_t, bf16[16,2,8,896]{3,2,1,0:T(8,128)(2,1)S(1)} %bitcast.83, bf16[16,2,8,896]{3,2,1,0:T(8,128)(2,1)S(1)} %collective-permute-done.12.other, ...), custom_call_target="tpu_custom_call" | custom-call | flops 234881024 | bytes 2752512 | tf_op jit(solution)/shard_map/grads_of_target/pallas_call | solution.py:71
  153.0 3.9 %grads_of_target.5 = (bf16[4,128,3584]{2,1,0:T(8,128)(2,1)}, f32[128,128]{1,0:T(8,128)S(1)}) custom-call(s32[3]{0:T(128)S(1)} %pad_add_fusion.2.places, bf16[128,128]{1,0:T(8,128)(2,1)S(1)} %copy.25.feats_t, bf16[16,2,8,896]{3,2,1,0:T(8,128)(2,1)} %collective-permute-done.10.own, ...), custom_call_target="tpu_custom_call", output_to_operand_aliasing={{0}: (6, {})} | custom-call | flops 234881024 | bytes 2752512 | tf_op jit(solution)/shard_map/grads_of_target/pallas_call | solution.py:71
  156.9 3.9 %grads_of_target.6 = (bf16[4,128,3584]{2,1,0:T(8,128)(2,1)}, f32[128,128]{1,0:T(8,128)S(1)}) custom-call(s32[3]{0:T(128)S(1)} %pad_add_fusion.1.places, bf16[128,128]{1,0:T(8,128)(2,1)S(1)} %copy.25.feats_t, bf16[16,2,8,896]{3,2,1,0:T(8,128)(2,1)} %collective-permute-done.8.own, ...), custom_call_target="tpu_custom_call", output_to_operand_aliasing={{0}: (6, {})} | custom-call | flops 234881024 | bytes 2752512 | tf_op jit(solution)/shard_map/grads_of_target/pallas_call | solution.py:71
  160.8 3.2 %grads_of_target.7 = (bf16[4,128,3584]{2,1,0:T(8,128)(2,1)}, f32[128,128]{1,0:T(8,128)S(1)}) custom-call(s32[3]{0:T(128)S(1)} %pad_add_fusion.places, bf16[128,128]{1,0:T(8,128)(2,1)S(1)} %copy.25.feats_t, bf16[16,2,8,896]{3,2,1,0:T(8,128)(2,1)S(1)} %collective-permute-done.6.own, ...), custom_call_target="tpu_custom_call", output_to_operand_aliasing={{0}: (6, {})} | custom-call | flops 234881024 | bytes 2752512 | tf_op jit(solution)/shard_map/grads_of_target/pallas_call | solution.py:71
  164.0 3.5 %encoder_grads.1 = (bf16[3584,128]{1,0:T(8,128)(2,1)}, f32[1,128]{1,0:T(1,128)}) custom-call(bf16[128,3584]{1,0:T(8,128)(2,1)S(1)} %reshape.57.acts, f32[128,128]{1,0:T(8,128)S(1)} %get-tuple-element.20.back, s32[128,128]{1,0:T(8,128)S(1)} %bitcast.84), custom_call_target="tpu_custom_call" | custom-call | flops 117440512 | bytes 1835008 | tf_op jit(solution)/shard_map/encoder_grads/pallas_call | solution.py:105
  (34 shorter events, 0.8 us)
Async XLA Ops:
  0.6 41.4 %copy-start = (bf16[1,3584,128]{2,1,0:T(8,128)(2,1)S(1)}, bf16[1,3584,128]{2,1,0:T(8,128)(2,1)}, u32[]{:S(2)}) copy-start(bf16[1,3584,128]{2,1,0:T(8,128)(2,1)} %param.8) | copy-start | bytes 2752516
  0.6 18.6 %copy-start.3 = (bf16[1,2,3584]{2,1,0:T(2,128)(2,1)S(1)}, bf16[1,2,3584]{2,1,0:T(2,128)(2,1)}, u32[]{:S(2)}) copy-start(bf16[1,2,3584]{2,1,0:T(2,128)(2,1)} %param.13) | copy-start | bytes 43012
  2.9 39.2 %copy-start.2 = (s32[1,128,128]{2,1,0:T(8,128)S(1)}, s32[1,128,128]{2,1,0:T(8,128)}, u32[]{:S(2)}) copy-start(s32[1,128,128]{2,1,0:T(8,128)} %param.10) | copy-start | bytes 196612
  2.9 39.2 %copy-start.4 = (f32[1,128]{1,0:T(1,128)S(1)}, f32[1,128]{1,0:T(1,128)}, u32[]{:S(2)}) copy-start(f32[1,128]{1,0:T(1,128)} %param.9) | copy-start | bytes 1540
  2.9 38.9 %all-to-all-start = ((bf16[64,2,3584]{2,1,0:T(2,128)(2,1)}), bf16[64,2,3584]{2,1,0:T(2,128)(2,1)S(1)}, u32[]{:S(2)}, u32[]{:S(2)}) async-start(bf16[64,2,3584]{2,1,0:T(2,128)(2,1)} %broadcast_in_dim.30), calls=%async_computation | async-start | bytes 1835008 | tf_op jit(solution)/shard_map/all_to_all | solution.py:146
  18.8 28.3 %collective-permute-start.1 = (bf16[4,128,1792]{2,1,0:T(8,128)(2,1)}, bf16[4,128,1792]{2,1,0:T(8,128)(2,1)}, u32[]{:S(2)}, u32[]{:S(2)}) collective-permute-start(bf16[4,128,1792]{2,1,0:T(8,128)(2,1)} %dynamic-slice_bitcast_fusion), channel_id=1, source_target_pairs={{0,1},{1,0},{2,3},{3,2},{4,5},{5,4},{6,7},{7,6},{8,9},{9,8},{10,11... | collective-permute-start | bytes 5505032 | tf_op jit(solution)/shard_map/ppermute | solution.py:134
  19.3 35.8 %collective-permute-start.2 = (bf16[2,1792]{1,0:T(2,128)(2,1)S(1)}, bf16[2,1792]{1,0:T(2,128)(2,1)S(1)}, u32[]{:S(2)}, u32[]{:S(2)}) collective-permute-start(bf16[2,1792]{1,0:T(2,128)(2,1)S(1)} %get-tuple-element.25), channel_id=1, source_target_pairs={{0,1},{1,0},{2,3},{3,2},{4,5},{5,4},{6,7},{7,6},{8,9},{9,8},{10,11... | collective-permute-start | bytes 21512 | tf_op jit(solution)/shard_map/ppermute | solution.py:137
  42.5 4.6 %collective-permute-start = (bf16[128,128]{1,0:T(8,128)(2,1)S(1)}, bf16[128,128]{1,0:T(8,128)(2,1)S(1)}, u32[]{:S(2)}, u32[]{:S(2)}) collective-permute-start(bf16[128,128]{1,0:T(8,128)(2,1)S(1)} %fusion.9), channel_id=1, source_target_pairs={{0,1},{1,0},{2,3},{3,2},{4,5},{5,4},{6,7},{7,6},{8,9},{9,8},{10,11... | collective-permute-start | bytes 98312 | tf_op jit(solution)/shard_map/ppermute | solution.py:150
  48.5 22.2 %collective-permute-start.3 = (bf16[128,1792]{1,0:T(8,128)(2,1)S(1)}, bf16[128,1792]{1,0:T(8,128)(2,1)S(1)}, u32[]{:S(2)}, u32[]{:S(2)}) collective-permute-start(bf16[128,1792]{1,0:T(8,128)(2,1)S(1)} %fusion.5), channel_id=1, source_target_pairs={{0,192},{64,0},{128,64},{192,128},{1,193},{65,1},{129,65},{193,129... | collective-permute-start | bytes 1376264 | tf_op jit(solution)/shard_map/ppermute | solution.py:162
  52.6 18.1 %collective-permute-start.4 = (bf16[128,1792]{1,0:T(8,128)(2,1)S(1)}, bf16[128,1792]{1,0:T(8,128)(2,1)S(1)}, u32[]{:S(2)}, u32[]{:S(2)}) collective-permute-start(bf16[128,1792]{1,0:T(8,128)(2,1)S(1)} %fusion.6), channel_id=1, source_target_pairs={{0,128},{64,192},{128,0},{192,64},{1,129},{65,193},{129,1},{193,65... | collective-permute-start | bytes 1376264 | tf_op jit(solution)/shard_map/ppermute | solution.py:162
  54.3 22.1 %collective-permute-start.5 = (bf16[128,1792]{1,0:T(8,128)(2,1)S(1)}, bf16[128,1792]{1,0:T(8,128)(2,1)S(1)}, u32[]{:S(2)}, u32[]{:S(2)}) collective-permute-start(bf16[128,1792]{1,0:T(8,128)(2,1)S(1)} %fusion.7), channel_id=1, source_target_pairs={{0,64},{64,128},{128,192},{192,0},{1,65},{65,129},{129,193},{193,1... | collective-permute-start | bytes 1376264 | tf_op jit(solution)/shard_map/ppermute | solution.py:162
  78.7 18.6 %all-to-all-start.1 = ((bf16[32,8,896]{2,1,0:T(8,128)(2,1)}), bf16[32,8,896]{2,1,0:T(8,128)(2,1)S(1)}, u32[]{:S(2)}, u32[]{:S(2)}) async-start(bf16[32,8,896]{2,1,0:T(8,128)(2,1)} %bitcast.21), calls=%async_computation.1 | async-start | bytes 917504 | tf_op jit(solution)/shard_map/all_to_all | solution.py:173
  98.1 19.9 %all-to-all-start.2 = ((bf16[32,8,896]{2,1,0:T(8,128)(2,1)}), bf16[32,8,896]{2,1,0:T(8,128)(2,1)S(1)}, u32[]{:S(2)}, u32[]{:S(2)}) async-start(bf16[32,8,896]{2,1,0:T(8,128)(2,1)} %broadcast_in_dim.32), calls=%async_computation.2 | async-start | bytes 917504 | tf_op jit(solution)/shard_map/all_to_all | solution.py:178
  118.1 6.6 %collective-permute-start.12 = (bf16[16,2,8,896]{3,2,1,0:T(8,128)(2,1)S(1)}, bf16[16,2,8,896]{3,2,1,0:T(8,128)(2,1)S(1)}, u32[]{:S(2)}, u32[]{:S(2)}) collective-permute-start(bf16[16,2,8,896]{3,2,1,0:T(8,128)(2,1)S(1)} %bitcast.79), channel_id=1, source_target_pairs={{0,1},{1,0},{2,3},{3,2},{4,5},{5,4},{6,7},{7,6},{8,9},{9,8},{10,11... | collective-permute-start | bytes 1376264 | tf_op jit(solution)/shard_map/ppermute | solution.py:185
  122.7 12.3 %collective-permute-start.10 = (bf16[16,2,8,896]{3,2,1,0:T(8,128)(2,1)S(1)}, bf16[16,2,8,896]{3,2,1,0:T(8,128)(2,1)}, u32[]{:S(2)}, u32[]{:S(2)}) collective-permute-start(bf16[16,2,8,896]{3,2,1,0:T(8,128)(2,1)S(1)} %bitcast.80), channel_id=1, source_target_pairs={{0,192},{64,0},{128,64},{192,128},{1,193},{65,1},{129,65},{193,129... | collective-permute-start | bytes 1376264 | tf_op jit(solution)/shard_map/ppermute | solution.py:180
  122.8 13.9 %collective-permute-start.8 = (bf16[16,2,8,896]{3,2,1,0:T(8,128)(2,1)S(1)}, bf16[16,2,8,896]{3,2,1,0:T(8,128)(2,1)}, u32[]{:S(2)}, u32[]{:S(2)}) collective-permute-start(bf16[16,2,8,896]{3,2,1,0:T(8,128)(2,1)S(1)} %bitcast.81), channel_id=1, source_target_pairs={{0,128},{64,192},{128,0},{192,64},{1,129},{65,193},{129,1},{193,65... | collective-permute-start | bytes 1376264 | tf_op jit(solution)/shard_map/ppermute | solution.py:180
  123.2 23.4 %collective-permute-start.6 = (bf16[16,2,8,896]{3,2,1,0:T(8,128)(2,1)S(1)}, bf16[16,2,8,896]{3,2,1,0:T(8,128)(2,1)S(1)}, u32[]{:S(2)}, u32[]{:S(2)}) collective-permute-start(bf16[16,2,8,896]{3,2,1,0:T(8,128)(2,1)S(1)} %bitcast.82), channel_id=1, source_target_pairs={{0,64},{64,128},{128,192},{192,0},{1,65},{65,129},{129,193},{193,1... | collective-permute-start | bytes 1376264 | tf_op jit(solution)/shard_map/ppermute | solution.py:180
  135.0 18.0 %collective-permute-start.11 = (bf16[16,2,8,896]{3,2,1,0:T(8,128)(2,1)}, bf16[16,2,8,896]{3,2,1,0:T(8,128)(2,1)S(1)}, u32[]{:S(2)}, u32[]{:S(2)}) collective-permute-start(bf16[16,2,8,896]{3,2,1,0:T(8,128)(2,1)} %collective-permute-done.10.own), channel_id=1, source_target_pairs={{0,1},{1,0},{2,3},{3,2},{4,5},{5,4},{6,7},{7,6},{8,9},{9,8},{10,11... | collective-permute-start | bytes 1376264 | tf_op jit(solution)/shard_map/ppermute | solution.py:185
  136.7 20.2 %collective-permute-start.9 = (bf16[16,2,8,896]{3,2,1,0:T(8,128)(2,1)}, bf16[16,2,8,896]{3,2,1,0:T(8,128)(2,1)S(1)}, u32[]{:S(2)}, u32[]{:S(2)}) collective-permute-start(bf16[16,2,8,896]{3,2,1,0:T(8,128)(2,1)} %collective-permute-done.8.own), channel_id=1, source_target_pairs={{0,1},{1,0},{2,3},{3,2},{4,5},{5,4},{6,7},{7,6},{8,9},{9,8},{10,11... | collective-permute-start | bytes 1376264 | tf_op jit(solution)/shard_map/ppermute | solution.py:185
  146.7 14.2 %collective-permute-start.7 = (bf16[16,2,8,896]{3,2,1,0:T(8,128)(2,1)S(1)}, bf16[16,2,8,896]{3,2,1,0:T(8,128)(2,1)S(1)}, u32[]{:S(2)}, u32[]{:S(2)}) collective-permute-start(bf16[16,2,8,896]{3,2,1,0:T(8,128)(2,1)S(1)} %collective-permute-done.6.own), channel_id=1, source_target_pairs={{0,1},{1,0},{2,3},{3,2},{4,5},{5,4},{6,7},{7,6},{8,9},{9,8},{10,11... | collective-permute-start | bytes 1376264 | tf_op jit(solution)/shard_map/ppermute | solution.py:185
  147.8 2.0 %copy-start.1 = (bf16[1,4,128,3584]{3,2,1,0:T(8,128)(2,1)S(1)}, bf16[1,4,128,3584]{3,2,1,0:T(8,128)(2,1)}, u32[]{:S(2)}) copy-start(bf16[1,4,128,3584]{3,2,1,0:T(8,128)(2,1)} %param.11) | copy-start | bytes 11010052

commit v2 on v0

v2 whole, which is shorter than its diff:
```python
import jax
import jax.numpy as jnp
from jax import lax
from jax.experimental import pallas as pl
from jax.experimental.pallas import tpu as pltpu
from jax.sharding import Mesh
from jax.sharding import PartitionSpec as P

SWAP = [(0, 1), (1, 0)]
BF16 = jnp.bfloat16
F32 = jnp.float32
PARAMS = pltpu.CompilerParams(vmem_limit_bytes=8 * 1024 * 1024)


def whole_block(*shape):
    return pl.BlockSpec(shape, lambda step, places: (0,) * len(shape))


def cost(flops, moved):
    return pl.CostEstimate(flops=flops, bytes_accessed=moved, transcendentals=0)


def swap_halves(block):
    middle = block.shape[0] // 2
    return jnp.concatenate([block[middle:], block[:middle]], axis=0)


def recon_kernel(places, feats, feats_other, mine, got, placed, out):
    target = pl.program_id(0)

    @pl.when(target < places[0])
    def _():
        out[...] = jnp.zeros_like(out)

    @pl.when(target >= places[0])
    def _():
        total = jnp.dot(feats[...], mine[0], preferred_element_type=F32) + jnp.dot(
            feats_other[...], got[0], preferred_element_type=F32
        )
        out[0] = total.astype(BF16)

        @pl.when(target == places[0])
        def _():
            out[0] = (total - placed[...].astype(F32)).astype(BF16)


def recon_partials(places, feats, feats_other, mine, got, placed):
    layers, latents, half = got.shape
    rows = feats.shape[0]
    return pl.pallas_call(
        recon_kernel,
        grid_spec=pltpu.PrefetchScalarGridSpec(
            num_scalar_prefetch=1,
            grid=(layers,),
            in_specs=[
                whole_block(rows, latents),
                whole_block(rows, latents),
                pl.BlockSpec((1, latents, half), lambda step, places: (step, 0, 0)),
                pl.BlockSpec((1, latents, half), lambda step, places: (step, 0, 0)),
                whole_block(rows, half),
            ],
            out_specs=pl.BlockSpec((1, rows, half), lambda step, places: (step, 0, 0)),
        ),
        out_shape=jax.ShapeDtypeStruct((layers, rows, half), BF16),
        compiler_params=PARAMS,
        cost_estimate=cost(4 * layers * rows * latents * half, 6 * layers * rows * half),
        name="recon_partials",
    )(places, feats, feats_other, mine, got, placed)


def add_kernel(pieces, out):
    total = jnp.sum(pieces[...].astype(F32), axis=0)
    quarter = out.shape[2]
    for group in range(total.shape[0] // 8):
        for side in range(2):
            tile = total[8 * group : 8 * group + 8, side * quarter : (side + 1) * quarter]
            out[2 * group + side] = tile.astype(BF16)


def add_pieces(pieces):
    count, rows, half = pieces.shape
    quarter = half // 2
    return pl.pallas_call(
        add_kernel,
        grid=(rows // 16,),
        in_specs=[pl.BlockSpec((count, 16, half), lambda step: (0, step, 0))],
        out_specs=pl.BlockSpec((4, 8, quarter), lambda step: (step, 0, 0)),
        out_shape=jax.ShapeDtypeStruct((rows // 4, 8, quarter), BF16),
        compiler_params=PARAMS,
        cost_estimate=cost(count * rows * half, 2 * count * rows * half),
        name="add_pieces",
    )(pieces)


def grads_kernel(places, feats_t, errs, decoder, *refs):
    grad_ref, back_ref, sums_ref = refs[-3:]
    target = pl.program_id(0)
    quarter = errs.shape[4]
    rows = feats_t.shape[1]

    @pl.when(target == 0)
    def _():
        back_ref[...] = jnp.zeros_like(back_ref)

    @pl.when(target < places[0])
    def _():
        grad_ref[...] = jnp.zeros_like(grad_ref)

    @pl.when(target >= places[0])
    def _():
        for side in range(2):
            lanes = slice(side * quarter, (side + 1) * quarter)
            tile = errs[0, :, side].reshape(rows, quarter)
            grad_ref[0, :, lanes] = jnp.dot(feats_t[...], tile, preferred_element_type=F32).astype(BF16)
            back_ref[...] += lax.dot_general(
                tile, decoder[0, :, lanes], (((1,), (1,)), ((), ())), preferred_element_type=F32
            )

            @pl.when(target == places[0])
            def _():
                sums_ref[:, lanes] = jnp.sum(tile.astype(F32), axis=0, keepdims=True)


def grads_of_half(places, feats_t, errs, decoder, carried):
    layers, latents, half = decoder.shape
    rows = feats_t.shape[1]
    width = 2 * half
    wide = pl.BlockSpec((1, latents, half), lambda step, places: (step, 0, places[1]))
    in_specs = [
        whole_block(latents, rows),
        pl.BlockSpec((1,) + errs.shape[1:], lambda step, places: (step, 0, 0, 0, 0)),
        pl.BlockSpec((1, latents, half), lambda step, places: (step, 0, 0)),
    ]
    operands = [places, feats_t, errs, decoder]
    aliases = {}
    if carried is not None:
        in_specs += [pl.BlockSpec(memory_space=pl.ANY)] * 2
        operands += list(carried)
        aliases = {4: 0, 5: 2}
    return pl.pallas_call(
        grads_kernel,
        grid_spec=pltpu.PrefetchScalarGridSpec(
            num_scalar_prefetch=1,
            grid=(layers,),
            in_specs=in_specs,
            out_specs=[
                wide,
                whole_block(rows, latents),
                pl.BlockSpec((1, half), lambda step, places: (0, places[1])),
            ],
        ),
        out_shape=[
            jax.ShapeDtypeStruct((layers, latents, width), BF16),
            jax.ShapeDtypeStruct((rows, latents), F32),
            jax.ShapeDtypeStruct((1, width), F32),
        ],
        input_output_aliases=aliases,
        compiler_params=PARAMS,
        cost_estimate=cost(4 * layers * rows * latents * half, 6 * layers * latents * half),
        name="grads_of_half",
    )(*operands)


def encoder_kernel(same, apart, back, back_other, gate, grad_ref, bias_ref):
    dpre = ((back[...] + swap_halves(back_other[...])) * gate[...].astype(F32)).astype(BF16)
    middle = same.shape[0]
    over_rows = (((0,), (0,)), ((), ()))
    grad = lax.dot_general(same[...], dpre[:middle], over_rows, preferred_element_type=F32)
    grad += lax.dot_general(apart[...], dpre[middle:], over_rows, preferred_element_type=F32)
    grad_ref[...] = grad.astype(BF16)
    bias_ref[...] = jnp.sum(dpre.astype(F32), axis=0, keepdims=True)


def encoder_grads(same, apart, back, back_other, active):
    middle, width = same.shape
    rows, latents = back.shape
    block = width // 2
    whole = pl.BlockSpec((rows, latents), lambda step: (0, 0))
    flat = pl.BlockSpec((middle, block), lambda step: (0, step))
    return pl.pallas_call(
        encoder_kernel,
        grid=(2,),
        in_specs=[flat, flat, whole, whole, whole],
        out_specs=[
            pl.BlockSpec((block, latents), lambda step: (step, 0)),
            pl.BlockSpec((1, latents), lambda step: (0, 0)),
        ],
        out_shape=[jax.ShapeDtypeStruct((width, latents), BF16), jax.ShapeDtypeStruct((1, latents), F32)],
        compiler_params=PARAMS,
        cost_estimate=cost(2 * rows * latents * width, 4 * latents * width),
        name="encoder_grads",
    )(same, apart, back, back_other, active)


def per_device(acts, enc_weight, enc_bias, active, dec_weight, dec_bias, targets):
    layer, core = lax.axis_index("y"), lax.axis_index("c")
    chip, place = lax.axis_index(("x", "z")), lax.axis_index("z")
    decoder = dec_weight[0]
    layers, latents, width = decoder.shape
    half, quarter = width // 2, width // 4
    rows = active.shape[1]
    held = acts.shape[1]
    chips = rows // (2 * held)
    scale = rows ** (-0.5)

    copies = jnp.broadcast_to(acts[0][None], (chips, held, width))
    same = lax.all_to_all(copies, ("x", "z"), 0, 0, tiled=True).reshape(chips * held, width)

    give = lax.dynamic_slice_in_dim(decoder, (1 - core) * half, half, axis=2)
    mine = lax.dynamic_slice_in_dim(decoder, core * half, half, axis=2)
    got = lax.ppermute(give, "c", SWAP)
    target_mine = lax.dynamic_slice_in_dim(targets[0], core * half, half, axis=1)
    target_give = lax.dynamic_slice_in_dim(targets[0], (1 - core) * half, half, axis=1)
    target_got = lax.ppermute(target_give, "c", SWAP)
    placed = jnp.zeros((rows, half), BF16)
    placed = lax.dynamic_update_slice_in_dim(placed, target_mine, chip * held, 0)
    placed = lax.dynamic_update_slice_in_dim(placed, target_got, rows // 2 + chip * held, 0)
    by_core = active[0].reshape(chips, 2, held, latents)
    active_rows = jnp.concatenate(
        [
            lax.dynamic_index_in_dim(by_core, which, 1, keepdims=False).reshape(rows // 2, latents)
            for which in (core, 1 - core)
        ],
        axis=0,
    )

    bias = lax.dynamic_slice(dec_bias, (layer, core * half + (place % 2) * quarter), (1, quarter))
    same, mine, bias, active_rows = lax.optimization_barrier((same, mine, bias, active_rows))
    apart = lax.ppermute(same, "c", SWAP)
    pre = jnp.concatenate(
        [jnp.dot(part, enc_weight[0], preferred_element_type=F32) for part in (same, apart)], axis=0
    )
    feats = ((pre + enc_bias[0][None, :]) * active_rows.astype(F32)).astype(BF16)
    feats_other = swap_halves(lax.ppermute(feats, "c", SWAP))

    places = jnp.stack([layer, core]).astype(jnp.int32)
    partials = recon_partials(places, feats, feats_other, mine, got, placed)
    pieces = lax.all_to_all(partials.reshape(16, rows // 4, half), ("y", "x"), 0, 0, tiled=True)
    chunks = lax.all_to_all(add_pieces(pieces), "z", 0, 0, tiled=True)
    summed = jnp.sum(chunks.astype(F32), axis=0)
    err = ((summed + bias) * scale).astype(BF16)
    near = lax.all_to_all(jnp.broadcast_to(err[None], chunks.shape), "z", 0, 0, tiled=True)
    far = lax.all_to_all(jnp.broadcast_to(near[None], (16,) + near.shape), ("y", "x"), 0, 0, tiled=True)
    errs = far.reshape(layers, rows // 8, 2, 8, quarter)
    errs_other = lax.ppermute(errs, "c", SWAP)

    feats_t, feats_t_other = feats.T, swap_halves(feats).T
    grads, back, sums = grads_of_half(places, feats_t, errs, mine, None)
    places_other = jnp.stack([layer, 1 - core]).astype(jnp.int32)
    grads, back_other, sums = grads_of_half(places_other, feats_t_other, errs_other, give, (grads, sums))
    grad_enc, grad_enc_bias = encoder_grads(same, apart, back, back_other, active_rows)
    return grad_enc[None], grad_enc_bias, grads[None], sums


def solution(mesh):
    split = Mesh(mesh.devices.reshape(4, 4, 8, 2), ("y", "x", "z", "c"))
    latent = ("x", "z", "c")
    return jax.shard_map(
        per_device,
        mesh=split,
        in_specs=(
            P("y", latent, None),
            P("y", None, latent),
            P("y", latent),
            P("y", None, latent),
            P("y", None, latent, None),
            P(),
            P("y", latent, None),
        ),
        out_specs=(
            P("y", None, latent),
            P("y", latent),
            P("y", None, latent, None),
            P("y", None),
        ),
        check_vma=False,
    )
```

time: 502 us -> 137 us (0.27)
  waiting for transfers between devices: 389 us -> 16.3 us
  starting transfers between devices: 0.08 us -> 25.2 us
  Pallas kernels: 0 us -> 18.6 us
  local copies, waits for them, and re-layouts: 24.9 us -> 8.69 us
  between operations: 14.1 us -> 0.82 us
  matrix products: 13.6 us -> 0.61 us
  blocking collectives: 55.4 us -> 65.8 us
    unnamed x3 -> x0, waiting for transfers between devices: 271 us -> none
    all_gather x1 -> x0, waiting for transfers between devices: 118 us -> none  [per_device(): lax.all_gather(err, ('layer', 'latent'), axis=0, tiled=True)]
    all_to_all x0 -> x3, blocking collectives: none -> 65.8 us  [the longest x1 30.2 us: per_device(): lax.all_to_all(partials.reshape(16, rows // 4, half), ('y', 'x'), 0, 0, t...]
    all_gather x1 -> x0, blocking collectives: 55.4 us -> none  [per_device(): whole = lax.all_gather(acts, 'latent', axis=1, tiled=True)[0]]
    pallas_call x0 -> x5, Pallas kernels: none -> 18.6 us  [the longest x2 11.9 us: grads_of_half(): pl.pallas_call(grads_kernel, grid_spec=pltpu.PrefetchScalarGridSpec(num_s...]
    all_to_all x0 -> x2, starting transfers between devices: none -> 15.5 us  [the longest x1 12 us: per_device(): lax.all_to_all(copies, ('x', 'z'), 0, 0, tiled=True)]
    all_to_all x0 -> x2, waiting for transfers between devices: none -> 14.4 us  [the longest x1 7.74 us: per_device(): chunks = lax.all_to_all(add_pieces(pieces), 'z', 0, 0, tiled=True)]
    reshape x2 -> x1, local copies, waits for them, and re-layouts: 14.4 us -> 1.19 us  [per_device(): lax.all_to_all(copies, ('x', 'z'), 0, 0, tiled=True)]
  transfers between devices with their start and end apart: 2 -> 7, of which waited for: 2 -> 4; matrix products, arithmetic and copies ran while one was open for 0% -> 5% of each run, Pallas kernels for 0% -> 4%
where the time goes in v2:
time: 137 us; the launch traced here: 136 us
  blocking collectives  65.8 us (48%)
  starting transfers between devices  25.2 us (18%)
  Pallas kernels  18.6 us (14%)
  waiting for transfers between devices  16.3 us (12%)
  local copies, waits for them, and re-layouts  8.69 us (6%)
    all_to_all x1, blocking collectives, per_device(): lax.all_to_all(partials.reshape(16, rows // 4, half), ('y', 'x'), 0, 0, t...  30.2 us
    all_to_all x1, blocking collectives, per_device(): lax.all_to_all(jnp.broadcast_to(near[None], (16,) + near.shape), ('y', 'x...  25.4 us
    all_to_all x1, starting transfers between devices, per_device(): lax.all_to_all(copies, ('x', 'z'), 0, 0, tiled=True)  12 us
    pallas_call x2, Pallas kernels, grads_of_half(): pl.pallas_call(grads_kernel, grid_spec=pltpu.PrefetchScalarGridSpec(num_s...  11.9 us
    all_to_all x1, blocking collectives, per_device(): lax.all_to_all(jnp.broadcast_to(err[None], chunks.shape), 'z', 0, 0, tile...  10.2 us
    all_to_all x1, waiting for transfers between devices, per_device(): chunks = lax.all_to_all(add_pieces(pieces), 'z', 0, 0, tiled=True)  7.74 us
    all_to_all x1, waiting for transfers between devices, per_device(): lax.all_to_all(copies, ('x', 'z'), 0, 0, tiled=True)  6.68 us
    ppermute x1, starting transfers between devices, per_device(): errs_other = lax.ppermute(errs, 'c', SWAP)  4.63 us
  transfers between devices with their start and end apart: 7, of which 4 were waited for; matrix products, arithmetic and copies ran while one was open for 5% of the time, Pallas kernels for 4%

profile of v2, /device:TPU:1, one launch (start us, length us, event | category | flops | bytes accessed | tf_op | source)
XLA Modules:
  0.0 136.2 jit_solution(14526930791412438618)
XLA Ops:
  0.6 0.0 copy-start
  0.6 1.8 %broadcast_in_dim.29 = bf16[32,2,3584]{2,1,0:T(2,128)(2,1)} broadcast(bf16[2,3584]{1,0:T(2,128)(2,1)} %bitcast.40), dimensions={1,2} | broadcast | bytes 473088 | tf_op jit(solution)/shard_map/broadcast_in_dim | solution.py:206
  2.4 12.0 %all-to-all-start = ((bf16[32,2,3584]{2,1,0:T(2,128)(2,1)}), bf16[32,2,3584]{2,1,0:T(2,128)(2,1)}, u32[]{:S(2)}, u32[]{:S(2)}) async-start(bf16[32,2,3584]{2,1,0:T(2,128)(2,1)} %broadcast_in_dim.29), calls=%async_computation | async-start | bytes 917504 | tf_op jit(solution)/shard_map/all_to_all | solution.py:207
  14.4 0.7 dynamic-slice_bitcast_fusion.2
  15.1 1.0 collective-permute-start.3
  16.1 0.0 copy-start.3
  16.1 0.0 copy-start.4
  16.1 3.6 %dynamic-slice_bitcast_fusion = (bf16[4,128,1792]{2,1,0:T(8,128)(2,1)}, bf16[4,128,1792]{2,1,0:T(8,128)(2,1)S(1)}) fusion(bf16[1,4,128,3584]{3,2,1,0:T(8,128)(2,1)} %param.11, s32[]{:T(128)S(6)} %select_n.40, s32[]{:T(128)S(6)} %select_n.34), kind=kLoop, calls=%fused_computation | loop fusion | bytes 7340040 | tf_op jit(solution)/shard_map/dynamic_slice | solution.py:209
  19.7 0.0 collective-permute-start.2
  19.7 0.8 dynamic_slice.32
  20.5 0.1 pad_add_fusion.1.places
  20.6 0.0 copy-done.3
  20.6 6.7 %all-to-all-done = bf16[32,2,3584]{2,1,0:T(2,128)(2,1)} async-done(((bf16[32,2,3584]{2,1,0:T(2,128)(2,1)}), bf16[32,2,3584]{2,1,0:T(2,128)(2,1)}, u32[]{:S(2)}, u32[]{:S(2)}) %all-to-all-start) | async-done | bytes 458784 | tf_op jit(solution)/shard_map/all_to_all | solution.py:207
  27.3 1.2 reshape.51.same
  28.5 0.0 copy-start.5
  28.5 3.5 %collective-permute-start = (bf16[64,3584]{1,0:T(8,128)(2,1)S(1)}, bf16[64,3584]{1,0:T(8,128)(2,1)S(1)}, u32[]{:S(2)}, u32[]{:S(2)}) collective-permute-start(bf16[64,3584]{1,0:T(8,128)(2,1)S(1)} %reshape.51.same), channel_id=1, source_target_pairs={{0,1},{1,0},{2,3},{3,2},{4,5},{5,4},{6,7},{7,6},{8,9},{9,8},{10,11... | collective-permute-start | bytes 1376264 | tf_op jit(solution)/shard_map/ppermute | solution.py:229
  32.1 0.0 copy-done.4
  32.2 0.0 copy-done
  32.2 0.3 fusion.2
  32.5 1.0 collective-permute-done.apart
  33.5 0.0 copy-start.1
  33.5 0.3 fusion
  33.8 0.0 copy-done.5
  33.9 0.5 collective-permute-start.1
  34.3 0.0 collective-permute-done.3
  34.4 0.8 collective-permute-done.1
  35.2 0.0 collective-permute-done.2.got
  35.2 3.9 %recon_partials.1 = bf16[4,128,1792]{2,1,0:T(8,128)(2,1)S(1)} custom-call(s32[2]{0:T(128)S(1)} %pad_add_fusion.1.places, bf16[128,128]{1,0:T(8,128)(2,1)S(1)} %fusion.5.feats, bf16[128,128]{1,0:T(8,128)(2,1)S(1)} %pad_maximum_fusion.feats_other, bf16[4,128,1792]{2,1,0:T(8,128)(2,1)S(1)} %get-tuple-element.18.mine.decoder, ...), custom_call_target="tpu_custom_call" | custom-call | flops 469762048 | bytes 5505024 | tf_op jit(solution)/shard_map/recon_partials/pallas_call | solution.py:50
  39.1 0.0 copy-done.1
  39.1 30.2 %all_to_all.25.pieces = bf16[16,32,1792]{2,1,0:T(8,128)(2,1)S(1)} all-to-all(bf16[16,32,1792]{2,1,0:T(8,128)(2,1)S(1)} %bitcast.34), channel_id=1, replica_groups=mesh['y'=4,'x'=4,'z'=8,'c'=2] {'y','x'}, dimensions={0} | all-to-all | bytes 3670016 | tf_op jit(solution)/shard_map/all_to_all | solution.py:238
  69.4 1.0 add_pieces.1
  70.4 3.6 %all-to-all-start.2 = ((bf16[8,8,896]{2,1,0:T(8,128)(2,1)}), bf16[8,8,896]{2,1,0:T(8,128)(2,1)S(1)}, u32[]{:S(2)}, u32[]{:S(2)}) async-start(bf16[8,8,896]{2,1,0:T(8,128)(2,1)} %add_pieces.1), calls=%async_computation.2 | async-start | bytes 229376 | tf_op jit(solution)/shard_map/all_to_all | solution.py:239
  74.0 7.7 %all-to-all-done.2 = bf16[8,8,896]{2,1,0:T(8,128)(2,1)S(1)} async-done(((bf16[8,8,896]{2,1,0:T(8,128)(2,1)}), bf16[8,8,896]{2,1,0:T(8,128)(2,1)S(1)}, u32[]{:S(2)}, u32[]{:S(2)}) %all-to-all-start.2) | async-done | bytes 114720 | tf_op jit(solution)/shard_map/all_to_all | solution.py:239
  81.8 10.2 %all_to_all.26 = bf16[8,8,896]{2,1,0:T(8,128)(2,1)S(1)} all-to-all(bf16[8,8,896]{2,1,0:T(8,128)(2,1)S(1)} %broadcast_in_dim.31), channel_id=1, replica_groups=mesh['y'=4,'x'=4,'z'=8,'c'=2] {'z'}, dimensions={0} | all-to-all | bytes 229376 | tf_op jit(solution)/shard_map/all_to_all | solution.py:242
  92.0 0.2 broadcast_in_dim.32
  92.2 25.4 %all_to_all.27 = bf16[16,8,8,896]{3,2,1,0:T(8,128)(2,1)} all-to-all(bf16[16,8,8,896]{3,2,1,0:T(8,128)(2,1)S(1)} %broadcast_in_dim.32), channel_id=1, replica_groups=mesh['y'=4,'x'=4,'z'=8,'c'=2] {'y','x'}, dimensions={0} | all-to-all | bytes 3670016 | tf_op jit(solution)/shard_map/all_to_all | solution.py:243
  117.6 4.6 %collective-permute-start.4 = (bf16[4,16,2,8,896]{4,3,2,1,0:T(8,128)(2,1)}, bf16[4,16,2,8,896]{4,3,2,1,0:T(8,128)(2,1)}, u32[]{:S(2)}, u32[]{:S(2)}) collective-permute-start(bf16[4,16,2,8,896]{4,3,2,1,0:T(8,128)(2,1)} %bitcast.14.errs), channel_id=1, source_target_pairs={{0,1},{1,0},{2,3},{3,2},{4,5},{5,4},{6,7},{7,6},{8,9},{9,8},{10,11... | collective-permute-start | bytes 5505032 | tf_op jit(solution)/shard_map/ppermute | solution.py:245
  122.2 0.1 pad_add_fusion.2.places
  122.3 0.1 copy.15.feats_t
  122.4 0.1 copy.16.feats_t
  122.5 5.8 %grads_of_half.2 = (bf16[4,128,3584]{2,1,0:T(8,128)(2,1)}, f32[128,128]{1,0:T(8,128)S(1)}, f32[1,3584]{1,0:T(1,128)}) custom-call(s32[2]{0:T(128)S(1)} %pad_add_fusion.1.places, bf16[128,128]{1,0:T(8,128)(2,1)S(1)} %copy.15.feats_t, bf16[4,16,2,8,896]{4,3,2,1,0:T(8,128)(2,1)} %bitcast.14.errs, bf16[4,128,1792]{2,1,0:T(8,128)(2,1)S(1)} %get-tuple-element.18.mine.decoder), custom_call_target="tpu_custom_call" | custom-call | flops 469762048 | bytes 5505024 | tf_op jit(solution)/shard_map/grads_of_half/pallas_call | solution.py:140
  128.3 0.0 collective-permute-done.4.errs
  128.3 0.0 copy-start.2
  128.3 6.1 %grads_of_half.3 = (bf16[4,128,3584]{2,1,0:T(8,128)(2,1)}, f32[128,128]{1,0:T(8,128)S(1)}, f32[1,3584]{1,0:T(1,128)}) custom-call(s32[2]{0:T(128)S(1)} %pad_add_fusion.2.places, bf16[128,128]{1,0:T(8,128)(2,1)S(1)} %copy.16.feats_t, bf16[4,16,2,8,896]{4,3,2,1,0:T(8,128)(2,1)} %collective-permute-done.4.errs, ...), custom_call_target="tpu_custom_call", output_to_operand_aliasing={{0}: (4, {}), {2}: (5, {})} | custom-call | flops 469762048 | bytes 5505024 | tf_op jit(solution)/shard_map/grads_of_half/pallas_call | solution.py:140
  134.4 0.0 copy-done.2
  134.4 1.8 %encoder_grads.1 = (bf16[3584,128]{1,0:T(8,128)(2,1)}, f32[1,128]{1,0:T(1,128)}) custom-call(bf16[64,3584]{1,0:T(8,128)(2,1)S(1)} %reshape.51.same, bf16[64,3584]{1,0:T(8,128)(2,1)S(1)} %copy-done.2, f32[128,128]{1,0:T(8,128)S(1)} %get-tuple-element.20.back, f32[128,128]{1,0:T(8,128)S(1)} %get-tuple-element.23.back_other, s32[128,128]{1,0:T(8,128)S(1)} %pad_add_fusion.gate), custom_call_target="tpu_custom_call" | custom-call | flops 117440512 | bytes 1835008 | tf_op jit(solution)/shard_map/encoder_grads/pallas_call | solution.py:180
  (14 shorter events, 0.2 us)
Async XLA Ops:
  0.6 31.5 %copy-start = (bf16[1,3584,128]{2,1,0:T(8,128)(2,1)S(1)}, bf16[1,3584,128]{2,1,0:T(8,128)(2,1)}, u32[]{:S(2)}) copy-start(bf16[1,3584,128]{2,1,0:T(8,128)(2,1)} %param.8) | copy-start | bytes 2752516
  2.4 24.9 %all-to-all-start = ((bf16[32,2,3584]{2,1,0:T(2,128)(2,1)}), bf16[32,2,3584]{2,1,0:T(2,128)(2,1)}, u32[]{:S(2)}, u32[]{:S(2)}) async-start(bf16[32,2,3584]{2,1,0:T(2,128)(2,1)} %broadcast_in_dim.29), calls=%async_computation | async-start | bytes 917504 | tf_op jit(solution)/shard_map/all_to_all | solution.py:207
  15.1 19.2 %collective-permute-start.3 = (bf16[2,1792]{1,0:T(2,128)(2,1)S(1)}, bf16[2,1792]{1,0:T(2,128)(2,1)S(1)}, u32[]{:S(2)}, u32[]{:S(2)}) collective-permute-start(bf16[2,1792]{1,0:T(2,128)(2,1)S(1)} %dynamic-slice_bitcast_fusion.2), channel_id=1, source_target_pairs={{0,1},{1,0},{2,3},{3,2},{4,5},{5,4},{6,7},{7,6},{8,9},{9,8},{10,11... | collective-permute-start | bytes 21512 | tf_op jit(solution)/shard_map/ppermute | solution.py:214
  16.1 4.5 %copy-start.3 = (s32[1,128,128]{2,1,0:T(8,128)S(1)}, s32[1,128,128]{2,1,0:T(8,128)}, u32[]{:S(2)}) copy-start(s32[1,128,128]{2,1,0:T(8,128)} %param.10) | copy-start | bytes 196612
  16.1 16.0 %copy-start.4 = (bf16[1,2,3584]{2,1,0:T(2,128)(2,1)S(1)}, bf16[1,2,3584]{2,1,0:T(2,128)(2,1)}, u32[]{:S(2)}) copy-start(bf16[1,2,3584]{2,1,0:T(2,128)(2,1)} %param.13) | copy-start | bytes 43012
  19.7 15.5 %collective-permute-start.2 = (bf16[4,128,1792]{2,1,0:T(8,128)(2,1)}, bf16[4,128,1792]{2,1,0:T(8,128)(2,1)}, u32[]{:S(2)}, u32[]{:S(2)}) collective-permute-start(bf16[4,128,1792]{2,1,0:T(8,128)(2,1)} %get-tuple-element.28.decoder), channel_id=1, source_target_pairs={{0,1},{1,0},{2,3},{3,2},{4,5},{5,4},{6,7},{7,6},{8,9},{9,8},{10,11... | collective-permute-start | bytes 5505032 | tf_op jit(solution)/shard_map/ppermute | solution.py:211
  28.5 5.3 %copy-start.5 = (f32[1,128]{1,0:T(1,128)S(1)}, f32[1,128]{1,0:T(1,128)}, u32[]{:S(2)}) copy-start(f32[1,128]{1,0:T(1,128)} %param.9) | copy-start | bytes 1540
  28.5 5.0 %collective-permute-start = (bf16[64,3584]{1,0:T(8,128)(2,1)S(1)}, bf16[64,3584]{1,0:T(8,128)(2,1)S(1)}, u32[]{:S(2)}, u32[]{:S(2)}) collective-permute-start(bf16[64,3584]{1,0:T(8,128)(2,1)S(1)} %reshape.51.same), channel_id=1, source_target_pairs={{0,1},{1,0},{2,3},{3,2},{4,5},{5,4},{6,7},{7,6},{8,9},{9,8},{10,11... | collective-permute-start | bytes 1376264 | tf_op jit(solution)/shard_map/ppermute | solution.py:229
  33.5 5.6 %copy-start.1 = (bf16[64,3584]{1,0:T(8,128)(2,1)}, bf16[64,3584]{1,0:T(8,128)(2,1)S(1)}, u32[]{:S(2)}) copy-start(bf16[64,3584]{1,0:T(8,128)(2,1)S(1)} %collective-permute-done.apart) | copy-start | bytes 1376260
  33.9 1.3 collective-permute-start.1
  70.4 11.3 %all-to-all-start.2 = ((bf16[8,8,896]{2,1,0:T(8,128)(2,1)}), bf16[8,8,896]{2,1,0:T(8,128)(2,1)S(1)}, u32[]{:S(2)}, u32[]{:S(2)}) async-start(bf16[8,8,896]{2,1,0:T(8,128)(2,1)} %add_pieces.1), calls=%async_computation.2 | async-start | bytes 229376 | tf_op jit(solution)/shard_map/all_to_all | solution.py:239
  117.6 10.7 %collective-permute-start.4 = (bf16[4,16,2,8,896]{4,3,2,1,0:T(8,128)(2,1)}, bf16[4,16,2,8,896]{4,3,2,1,0:T(8,128)(2,1)}, u32[]{:S(2)}, u32[]{:S(2)}) collective-permute-start(bf16[4,16,2,8,896]{4,3,2,1,0:T(8,128)(2,1)} %bitcast.14.errs), channel_id=1, source_target_pairs={{0,1},{1,0},{2,3},{3,2},{4,5},{5,4},{6,7},{7,6},{8,9},{9,8},{10,11... | collective-permute-start | bytes 5505032 | tf_op jit(solution)/shard_map/ppermute | solution.py:245
  128.3 6.1 %copy-start.2 = (bf16[64,3584]{1,0:T(8,128)(2,1)S(1)}, bf16[64,3584]{1,0:T(8,128)(2,1)}, u32[]{:S(2)}) copy-start(bf16[64,3584]{1,0:T(8,128)(2,1)} %copy-done.1) | copy-start | bytes 1376260

commit v3 on v2

v3 whole, which is shorter than its diff:
```python
import jax
import jax.numpy as jnp
from jax import lax
from jax.experimental import pallas as pl
from jax.experimental.pallas import tpu as pltpu
from jax.sharding import Mesh
from jax.sharding import PartitionSpec as P

SWAP = [(0, 1), (1, 0)]
BF16 = jnp.bfloat16
F32 = jnp.float32
VMEM = pl.BlockSpec(memory_space=pltpu.VMEM)
SMEM = pl.BlockSpec(memory_space=pltpu.SMEM)
ANY = pl.BlockSpec(memory_space=pl.ANY)
OVER_ROWS = (((0,), (0,)), ((), ()))


def params(mebibytes):
    return pltpu.CompilerParams(vmem_limit_bytes=mebibytes * 1024 * 1024)


def cost(flops, moved):
    return pl.CostEstimate(flops=flops, bytes_accessed=moved, transcendentals=0)


def swap_halves(block):
    middle = block.shape[0] // 2
    return jnp.concatenate([block[middle:], block[:middle]], axis=0)


def start_all(source, held, sems):
    copies = [pltpu.make_async_copy(source.at[i], held.at[i], sems.at[i]) for i in range(held.shape[0])]
    for copy in copies:
        copy.start()
    return copies


def half_of(source, side, held):
    half = held.shape[2]
    return source.at[:, :, pl.ds(pl.multiple_of(side * half, half), half)]


def recon_kernel(layer, feats, feats_other, mine, got, placed, out, held, out_held, mine_sems, got_sems, out_sems):
    layers, rows, _ = out_held.shape
    latents = feats.shape[1]
    loads = []
    for target in range(layers):
        for which, (source, sems) in enumerate(((mine, mine_sems), (got, got_sems))):
            place = held.at[target, pl.ds(which * latents, latents)]
            loads.append(pltpu.make_async_copy(source.at[target], place, sems.at[target]))
            loads[-1].start()
    leaving = [pltpu.make_async_copy(out_held.at[t], out.at[t], out_sems.at[t]) for t in range(layers)]
    both = jnp.concatenate([feats[...], swap_halves(feats_other[...])], axis=1)
    for target in range(layers):
        loads[2 * target].wait()
        loads[2 * target + 1].wait()

        @pl.when(target < layer[0])
        def _():
            out_held[target] = jnp.zeros(out_held.shape[1:], BF16)

        @pl.when(target > layer[0])
        def _():
            out_held[target] = jnp.dot(both, held[target], preferred_element_type=F32).astype(BF16)

        @pl.when(target == layer[0])
        def _():
            total = jnp.dot(both, held[target], preferred_element_type=F32)
            out_held[target] = (total - placed[...].astype(F32)).astype(BF16)

        leaving[target].start()
    for copy in leaving:
        copy.wait()


def recon_partials(layer, feats, feats_other, mine, got, placed):
    layers, latents, half = got.shape
    rows = feats.shape[0]
    sems = pltpu.SemaphoreType.DMA((layers,))
    return pl.pallas_call(
        recon_kernel,
        in_specs=[SMEM, VMEM, VMEM, ANY, ANY, VMEM],
        out_specs=ANY,
        out_shape=jax.ShapeDtypeStruct((layers, rows, half), BF16),
        scratch_shapes=[
            pltpu.VMEM((layers, 2 * latents, half), BF16),
            pltpu.VMEM((layers, rows, half), BF16),
            sems,
            sems,
            sems,
        ],
        compiler_params=params(14),
        cost_estimate=cost(4 * layers * rows * latents * half, 6 * layers * rows * half),
        name="recon_partials",
    )(layer, feats, feats_other, mine, got, placed)


def add_kernel(pieces, out):
    total = jnp.sum(pieces[...].astype(F32), axis=0)
    quarter = out.shape[2]
    for group in range(total.shape[0] // 8):
        for side in range(2):
            tile = total[8 * group : 8 * group + 8, side * quarter : (side + 1) * quarter]
            out[2 * group + side] = tile.astype(BF16)


def add_pieces(pieces):
    count, rows, half = pieces.shape
    quarter = half // 2
    return pl.pallas_call(
        add_kernel,
        grid=(rows // 16,),
        in_specs=[pl.BlockSpec((count, 16, half), lambda step: (0, step, 0))],
        out_specs=pl.BlockSpec((4, 8, quarter), lambda step: (step, 0, 0)),
        out_shape=jax.ShapeDtypeStruct((rows // 4, 8, quarter), BF16),
        compiler_params=params(8),
        cost_estimate=cost(count * rows * half, 2 * count * rows * half),
        name="add_pieces",
    )(pieces)


def half_of_targets(layer, side, feats, err_of, decoder_of, grads, held, sems, total, sums):
    layers, latents, half = held.shape
    quarter = half // 2
    rows = feats.shape[0]
    lanes = pl.ds(pl.multiple_of(side * half, half), half)
    leaving = [pltpu.make_async_copy(held.at[t], grads.at[t, :, lanes], sems.at[t]) for t in range(layers)]

    def tile(target, part):
        return err_of(target)[:, part].reshape(rows, quarter)

    for target in range(layers):
        err_of(target, wait=True)

        @pl.when(target < layer)
        def _():
            held[target] = jnp.zeros(held.shape[1:], BF16)

        @pl.when(target >= layer)
        def _():
            for part in range(2):
                held[target, :, part * quarter : (part + 1) * quarter] = lax.dot_general(
                    feats, tile(target, part), OVER_ROWS, preferred_element_type=F32
                ).astype(BF16)

        leaving[target].start()
    total[...] = jnp.zeros_like(total)
    for target in range(layers):
        decoder_of(target, wait=True)

        @pl.when(target >= layer)
        def _():
            for part in range(2):
                total[...] += lax.dot_general(
                    tile(target, part),
                    decoder_of(target)[:, part * quarter : (part + 1) * quarter],
                    (((1,), (1,)), ((), ())),
                    preferred_element_type=F32,
                )

        @pl.when(target == layer)
        def _():
            for part in range(2):
                sums[:, part * quarter : (part + 1) * quarter] = jnp.sum(
                    tile(target, part).astype(F32), axis=0, keepdims=True
                )

    return leaving


def own_half_kernel(places, feats, errs, decoder, grads, back, sums, decoder_held, held, decoder_sems, sems):
    loads = start_all(half_of(decoder, places[1], decoder_held), decoder_held, decoder_sems)

    def decoder_of(target, wait=False):
        if wait:
            loads[target].wait()
        return decoder_held.at[target]

    def err_of(target, wait=False):
        return errs.at[target]

    leaving = half_of_targets(places[0], places[1], feats[...], err_of, decoder_of, grads, held, sems, back, sums)
    for copy in leaving:
        copy.wait()


def own_half(places, feats, errs, decoder):
    layers, latents, width = decoder.shape
    half = width // 2
    rows = feats.shape[0]
    block = pltpu.VMEM((layers, latents, half), BF16)
    sems = pltpu.SemaphoreType.DMA((layers,))
    return pl.pallas_call(
        own_half_kernel,
        in_specs=[SMEM, VMEM, VMEM, ANY],
        out_specs=[ANY, VMEM, VMEM],
        out_shape=[
            jax.ShapeDtypeStruct((layers, latents, 2 * half), BF16),
            jax.ShapeDtypeStruct((rows, latents), F32),
            jax.ShapeDtypeStruct((1, half), F32),
        ],
        scratch_shapes=[block, block, sems, sems],
        compiler_params=params(14),
        cost_estimate=cost(4 * layers * rows * latents * half, 6 * layers * latents * half),
        name="own_half",
    )(places, feats, errs, decoder)


def other_half_kernel(
    places, feats, gate, back, own_sums, errs, decoder, same, apart, grads_in,
    grads, sums, grad_enc, enc_sums,
    decoder_held, held, enc_held, total, other_sums, decoder_sems, sems, enc_sems,
):
    loads = start_all(half_of(decoder, 1 - places[1], decoder_held), decoder_held, decoder_sems)

    def err_of(target, wait=False):
        return errs.at[target]

    def decoder_of(target, wait=False):
        if wait:
            loads[target].wait()
        return decoder_held.at[target]

    leaving = half_of_targets(
        places[0], 1 - places[1], swap_halves(feats[...]), err_of, decoder_of, grads, held, sems, total, other_sums
    )
    dpre = ((back[...] + swap_halves(total[...])) * gate[...].astype(F32)).astype(BF16)
    enc_sums[...] = jnp.sum(dpre.astype(F32), axis=0, keepdims=True)
    parts, block, _ = enc_held.shape
    middle = same.shape[0]
    for part in range(parts):
        lanes = slice(part * block, (part + 1) * block)
        enc_held[part] = (
            lax.dot_general(same[:, lanes], dpre[:middle], OVER_ROWS, preferred_element_type=F32)
            + lax.dot_general(apart[:, lanes], dpre[middle:], OVER_ROWS, preferred_element_type=F32)
        ).astype(BF16)
        copy = pltpu.make_async_copy(enc_held.at[part], grad_enc.at[pl.ds(part * block, block)], enc_sems.at[part])
        copy.start()
        leaving.append(copy)
    half = own_sums.shape[1]

    @pl.when(places[1] == 0)
    def _():
        sums[:, :half] = own_sums[...]
        sums[:, half:] = other_sums[...]

    @pl.when(places[1] == 1)
    def _():
        sums[:, :half] = other_sums[...]
        sums[:, half:] = own_sums[...]

    for copy in leaving:
        copy.wait()


def other_half(places, feats, gate, back, own_sums, errs, decoder, same, apart, grads):
    layers, latents, width = decoder.shape
    rows, half = feats.shape[0], width // 2
    block = pltpu.VMEM((layers, latents, half), BF16)
    sems = pltpu.SemaphoreType.DMA((layers,))
    return pl.pallas_call(
        other_half_kernel,
        in_specs=[SMEM, VMEM, VMEM, VMEM, VMEM, VMEM, ANY, VMEM, VMEM, ANY],
        out_specs=[ANY, VMEM, ANY, VMEM],
        out_shape=[
            jax.ShapeDtypeStruct(grads.shape, BF16),
            jax.ShapeDtypeStruct((1, width), F32),
            jax.ShapeDtypeStruct((width, latents), BF16),
            jax.ShapeDtypeStruct((1, latents), F32),
        ],
        scratch_shapes=[
            block,
            block,
            pltpu.VMEM((4, width // 4, latents), BF16),
            pltpu.VMEM((rows, latents), F32),
            pltpu.VMEM((1, half), F32),
            sems,
            sems,
            sems,
        ],
        input_output_aliases={9: 0},
        compiler_params=params(20),
        cost_estimate=cost(6 * layers * rows * latents * half, 8 * layers * latents * half),
        name="other_half",
    )(places, feats, gate, back, own_sums, errs, decoder, same, apart, grads)


def per_device(acts, enc_weight, enc_bias, active, dec_weight, dec_bias, targets):
    layer, core = lax.axis_index("y"), lax.axis_index("c")
    chip, place = lax.axis_index(("x", "z")), lax.axis_index("z")
    decoder = dec_weight[0]
    layers, latents, width = decoder.shape
    half, quarter = width // 2, width // 4
    rows = active.shape[1]
    held = acts.shape[1]
    chips = rows // (2 * held)
    scale = rows ** (-0.5)

    copies = jnp.broadcast_to(acts[0][None], (chips, held, width))
    same = lax.all_to_all(copies, ("x", "z"), 0, 0, tiled=True).reshape(chips * held, width)

    give = lax.dynamic_slice_in_dim(decoder, (1 - core) * half, half, axis=2)
    mine = lax.dynamic_slice_in_dim(decoder, core * half, half, axis=2)
    got = lax.ppermute(give, "c", SWAP)
    target_mine = lax.dynamic_slice_in_dim(targets[0], core * half, half, axis=1)
    target_give = lax.dynamic_slice_in_dim(targets[0], (1 - core) * half, half, axis=1)
    target_got = lax.ppermute(target_give, "c", SWAP)
    placed = jnp.zeros((rows, half), BF16)
    placed = lax.dynamic_update_slice_in_dim(placed, target_mine, chip * held, 0)
    placed = lax.dynamic_update_slice_in_dim(placed, target_got, rows // 2 + chip * held, 0)
    by_core = active[0].reshape(chips, 2, held, latents)
    active_rows = jnp.concatenate(
        [
            lax.dynamic_index_in_dim(by_core, which, 1, keepdims=False).reshape(rows // 2, latents)
            for which in (core, 1 - core)
        ],
        axis=0,
    )

    bias = lax.dynamic_slice(dec_bias, (layer, core * half + (place % 2) * quarter), (1, quarter))[0]
    same, mine, bias, active_rows = lax.optimization_barrier((same, mine, bias, active_rows))
    apart = lax.ppermute(same, "c", SWAP)
    pre = jnp.concatenate(
        [jnp.dot(part, enc_weight[0], preferred_element_type=F32) for part in (same, apart)], axis=0
    )
    feats = ((pre + enc_bias[0][None, :]) * active_rows.astype(F32)).astype(BF16)
    feats_other = lax.ppermute(feats, "c", SWAP)

    places = jnp.stack([layer, core]).astype(jnp.int32)
    partials = recon_partials(places, feats, feats_other, mine, got, placed)
    pieces = lax.all_to_all(partials.reshape(16, rows // 4, half), ("y", "x"), 0, 0, tiled=True)
    chunks = lax.all_to_all(add_pieces(pieces), "z", 0, 0, tiled=True)
    summed = jnp.sum(chunks.astype(F32), axis=0)
    err = ((summed + bias) * scale).astype(BF16)
    near = lax.all_to_all(jnp.broadcast_to(err[None], chunks.shape), "z", 0, 0, tiled=True)
    far = lax.all_to_all(jnp.broadcast_to(near[None], (16,) + near.shape), ("y", "x"), 0, 0, tiled=True)
    errs = far.reshape(layers, rows // 8, 2, 8, quarter)
    errs_other = lax.ppermute(errs, "c", SWAP)

    grads, back, own_sums = own_half(places, feats, errs, decoder)
    grads, sums, grad_enc, grad_enc_bias = other_half(
        places, feats, active_rows, back, own_sums, errs_other, decoder, same, apart, grads
    )
    return grad_enc[None], grad_enc_bias, grads[None], sums


def solution(mesh):
    split = Mesh(mesh.devices.reshape(4, 4, 8, 2), ("y", "x", "z", "c"))
    latent = ("x", "z", "c")
    return jax.shard_map(
        per_device,
        mesh=split,
        in_specs=(
            P("y", latent, None),
            P("y", None, latent),
            P("y", latent),
            P("y", None, latent),
            P("y", None, latent, None),
            P(),
            P("y", latent, None),
        ),
        out_specs=(
            P("y", None, latent),
            P("y", latent),
            P("y", None, latent, None),
            P("y", None),
        ),
        check_vma=False,
    )
```

time: 137 us -> 131 us (0.956)
  blocking collectives: 65.8 us -> 77 us
  waiting for transfers between devices: 16.3 us -> 9.26 us
  Pallas kernels: 18.6 us -> 13.4 us
  starting transfers between devices: 25.2 us -> 21.5 us
    all_to_all x0 -> x1, blocking collectives: none -> 11.1 us  [per_device(): chunks = lax.all_to_all(add_pieces(pieces), 'z', 0, 0, tiled=True)]
    all_to_all x1 -> x0, waiting for transfers between devices: 7.74 us -> none  [per_device(): chunks = lax.all_to_all(add_pieces(pieces), 'z', 0, 0, tiled=True)]
    pallas_call x4 -> x3, Pallas kernels: 17.6 us -> 13 us  [the longest x1 5.41 us: other_half(): pl.pallas_call(other_half_kernel, in_specs=[SMEM, VMEM, VMEM, VMEM, VMEM,...]
    all_to_all x1 -> x0, starting transfers between devices: 3.57 us -> none  [per_device(): chunks = lax.all_to_all(add_pieces(pieces), 'z', 0, 0, tiled=True)]
  transfers between devices with their start and end apart: 7 -> 6, of which waited for: 4 -> 4; matrix products, arithmetic and copies ran while one was open for 5% -> 5% of each run, Pallas kernels for 4% -> 3%
where the time goes in v3:
time: 131 us
  blocking collectives  77 us (59%)
  starting transfers between devices  21.5 us (16%)
  Pallas kernels  13.4 us (10%)
  waiting for transfers between devices  9.26 us (7%)
  local copies, waits for them, and re-layouts  7.75 us (6%)
    all_to_all x1, blocking collectives, per_device(): lax.all_to_all(partials.reshape(16, rows // 4, half), ('y', 'x'), 0, 0, t...  30.1 us
    all_to_all x1, blocking collectives, per_device(): lax.all_to_all(jnp.broadcast_to(near[None], (16,) + near.shape), ('y', 'x...  25.6 us
    all_to_all x1, starting transfers between devices, per_device(): lax.all_to_all(copies, ('x', 'z'), 0, 0, tiled=True)  12 us
    all_to_all x1, blocking collectives, per_device(): chunks = lax.all_to_all(add_pieces(pieces), 'z', 0, 0, tiled=True)  11.1 us
    all_to_all x1, blocking collectives, per_device(): lax.all_to_all(jnp.broadcast_to(err[None], chunks.shape), 'z', 0, 0, tile...  10.2 us
    all_to_all x1, waiting for transfers between devices, per_device(): lax.all_to_all(copies, ('x', 'z'), 0, 0, tiled=True)  7.27 us
    pallas_call x1, Pallas kernels, other_half(): pl.pallas_call(other_half_kernel, in_specs=[SMEM, VMEM, VMEM, VMEM, VMEM,...  5.41 us
    ppermute x1, starting transfers between devices, per_device(): errs_other = lax.ppermute(errs, 'c', SWAP)  4.47 us
  transfers between devices with their start and end apart: 6, of which 4 were waited for; matrix products, arithmetic and copies ran while one was open for 5% of the time, Pallas kernels for 3%

profile of v3, /device:TPU:1, one launch (start us, length us, event | category | flops | bytes accessed | tf_op | source)
XLA Modules:
  0.0 130.5 jit_solution(9137459728021325279)
XLA Ops:
  0.6 0.0 copy-start
  0.6 1.8 %broadcast_in_dim.30 = bf16[32,2,3584]{2,1,0:T(2,128)(2,1)} broadcast(bf16[2,3584]{1,0:T(2,128)(2,1)} %bitcast.40), dimensions={1,2} | broadcast | bytes 473088 | tf_op jit(solution)/shard_map/broadcast_in_dim | solution.py:299
  2.4 12.0 %all-to-all-start = ((bf16[32,2,3584]{2,1,0:T(2,128)(2,1)}), bf16[32,2,3584]{2,1,0:T(2,128)(2,1)}, u32[]{:S(2)}, u32[]{:S(2)}) async-start(bf16[32,2,3584]{2,1,0:T(2,128)(2,1)} %broadcast_in_dim.30), calls=%async_computation | async-start | bytes 917504 | tf_op jit(solution)/shard_map/all_to_all | solution.py:300
  14.4 0.0 copy-start.3
  14.5 0.0 copy-start.2
  14.5 3.6 %dynamic-slice_bitcast_fusion = (bf16[4,128,1792]{2,1,0:T(8,128)(2,1)}, bf16[4,128,1792]{2,1,0:T(8,128)(2,1)S(1)}) fusion(bf16[1,4,128,3584]{3,2,1,0:T(8,128)(2,1)} %param.11, s32[]{:T(128)S(6)} %select_n.40, s32[]{:T(128)S(6)} %select_n.34), kind=kLoop, calls=%fused_computation | loop fusion | bytes 7340040 | tf_op jit(solution)/shard_map/dynamic_slice | solution.py:302
  18.0 1.0 collective-permute-start.2
  19.0 0.0 copy-done.3
  19.0 0.1 collective-permute-start.3
  19.1 0.8 dynamic-slice_reduce_fusion
  19.9 0.1 pad_add_fusion.1.layer.places
  20.0 0.0 copy-done.2
  20.1 7.3 %all-to-all-done = bf16[32,2,3584]{2,1,0:T(2,128)(2,1)} async-done(((bf16[32,2,3584]{2,1,0:T(2,128)(2,1)}), bf16[32,2,3584]{2,1,0:T(2,128)(2,1)}, u32[]{:S(2)}, u32[]{:S(2)}) %all-to-all-start) | async-done | bytes 458784 | tf_op jit(solution)/shard_map/all_to_all | solution.py:300
  27.3 1.2 reshape.50.same
  28.5 0.0 copy-start.4
  28.5 3.5 %collective-permute-start = (bf16[64,3584]{1,0:T(8,128)(2,1)S(1)}, bf16[64,3584]{1,0:T(8,128)(2,1)S(1)}, u32[]{:S(2)}, u32[]{:S(2)}) collective-permute-start(bf16[64,3584]{1,0:T(8,128)(2,1)S(1)} %reshape.50.same), channel_id=1, source_target_pairs={{0,1},{1,0},{2,3},{3,2},{4,5},{5,4},{6,7},{7,6},{8,9},{9,8},{10,11... | collective-permute-start | bytes 1376264 | tf_op jit(solution)/shard_map/ppermute | solution.py:322
  32.1 0.0 copy-done
  32.2 0.3 fusion.2
  32.5 1.1 collective-permute-done.apart
  33.5 0.3 fusion
  33.8 0.0 copy-done.4
  33.9 0.5 collective-permute-start.1
  34.3 0.0 collective-permute-done.3
  34.3 0.8 collective-permute-done.1.feats_other
  35.2 0.0 collective-permute-done.2.got
  35.2 4.3 %recon_partials.1 = bf16[4,128,1792]{2,1,0:T(8,128)(2,1)S(1)} custom-call(s32[2]{0:T(128)S(1)} %pad_add_fusion.1.layer.places, bf16[128,128]{1,0:T(8,128)(2,1)S(1)} %fusion.5.feats, bf16[128,128]{1,0:T(8,128)(2,1)S(1)} %collective-permute-done.1.feats_other, bf16[4,128,1792]{2,1,0:T(8,128)(2,1)S(1)} %get-tuple-element.17.mine, ...), custom_call_target="tpu_custom_call" | custom-call | flops 469762048 | bytes 5505024 | tf_op jit(solution)/shard_map/recon_partials/pallas_call | solution.py:80
  39.5 30.1 %all_to_all.25.pieces = bf16[16,32,1792]{2,1,0:T(8,128)(2,1)S(1)} all-to-all(bf16[16,32,1792]{2,1,0:T(8,128)(2,1)S(1)} %bitcast.35), channel_id=1, replica_groups=mesh['y'=4,'x'=4,'z'=8,'c'=2] {'y','x'}, dimensions={0} | all-to-all | bytes 3670016 | tf_op jit(solution)/shard_map/all_to_all | solution.py:331
  69.5 0.4 add_pieces.1
  70.0 11.1 %all_to_all.26 = bf16[8,8,896]{2,1,0:T(8,128)(2,1)S(1)} all-to-all(bf16[8,8,896]{2,1,0:T(8,128)(2,1)S(1)} %add_pieces.1), channel_id=1, replica_groups=mesh['y'=4,'x'=4,'z'=8,'c'=2] {'z'}, dimensions={0} | all-to-all | bytes 229376 | tf_op jit(solution)/shard_map/all_to_all | solution.py:332
  81.1 10.2 %all_to_all.27 = bf16[8,8,896]{2,1,0:T(8,128)(2,1)S(1)} all-to-all(bf16[8,8,896]{2,1,0:T(8,128)(2,1)S(1)} %broadcast_in_dim.32), channel_id=1, replica_groups=mesh['y'=4,'x'=4,'z'=8,'c'=2] {'z'}, dimensions={0} | all-to-all | bytes 229376 | tf_op jit(solution)/shard_map/all_to_all | solution.py:335
  91.3 0.2 broadcast_in_dim.33
  91.6 0.0 copy-start.1
  91.6 25.6 %all_to_all.28 = bf16[16,8,8,896]{3,2,1,0:T(8,128)(2,1)S(1)} all-to-all(bf16[16,8,8,896]{3,2,1,0:T(8,128)(2,1)S(1)} %broadcast_in_dim.33), channel_id=1, replica_groups=mesh['y'=4,'x'=4,'z'=8,'c'=2] {'y','x'}, dimensions={0} | all-to-all | bytes 3670016 | tf_op jit(solution)/shard_map/all_to_all | solution.py:336
  117.2 4.5 %collective-permute-start.4 = (bf16[4,16,2,8,896]{4,3,2,1,0:T(8,128)(2,1)S(1)}, bf16[4,16,2,8,896]{4,3,2,1,0:T(8,128)(2,1)S(1)}, u32[]{:S(2)}, u32[]{:S(2)}) collective-permute-start(bf16[4,16,2,8,896]{4,3,2,1,0:T(8,128)(2,1)S(1)} %bitcast.33), channel_id=1, source_target_pairs={{0,1},{1,0},{2,3},{3,2},{4,5},{5,4},{6,7},{7,6},{8,9},{9,8},{10,11... | collective-permute-start | bytes 5505032 | tf_op jit(solution)/shard_map/ppermute | solution.py:338
  121.7 0.0 copy-done.1
  121.7 3.3 %own_half.1 = (bf16[4,128,3584]{2,1,0:T(8,128)(2,1)}, f32[128,128]{1,0:T(8,128)S(1)}, f32[1,1792]{1,0:T(1,128)S(1)}) custom-call(s32[2]{0:T(128)S(1)} %pad_add_fusion.1.layer.places, bf16[128,128]{1,0:T(8,128)(2,1)S(1)} %fusion.5.feats, bf16[4,16,2,8,896]{4,3,2,1,0:T(8,128)(2,1)S(1)} %bitcast.34, bf16[4,128,3584]{2,1,0:T(8,128)(2,1)S(1)} %bitcast.31), custom_call_target="tpu_custom_call" | custom-call | flops 469762048 | bytes 5505024 | tf_op jit(solution)/shard_map/own_half/pallas_call | solution.py:193
  125.0 0.1 collective-permute-done.4.errs
  125.1 5.4 %other_half.1 = (bf16[4,128,3584]{2,1,0:T(8,128)(2,1)}, f32[1,3584]{1,0:T(1,128)}, bf16[3584,128]{1,0:T(8,128)(2,1)}, f32[1,128]{1,0:T(1,128)}) custom-call(s32[2]{0:T(128)S(1)} %pad_add_fusion.1.layer.places, bf16[128,128]{1,0:T(8,128)(2,1)S(1)} %fusion.5.feats, s32[128,128]{1,0:T(8,128)S(1)} %pad_add_fusion.gate, ...), custom_call_target="tpu_custom_call", output_to_operand_aliasing={{0}: (9, {})} | custom-call | flops 704643072 | bytes 7340032 | tf_op jit(solution)/shard_map/other_half/pallas_call | solution.py:261
  (10 shorter events, 0.2 us)
Async XLA Ops:
  0.6 31.5 %copy-start = (bf16[1,3584,128]{2,1,0:T(8,128)(2,1)S(1)}, bf16[1,3584,128]{2,1,0:T(8,128)(2,1)}, u32[]{:S(2)}) copy-start(bf16[1,3584,128]{2,1,0:T(8,128)(2,1)} %param.8) | copy-start | bytes 2752516
  2.4 24.9 %all-to-all-start = ((bf16[32,2,3584]{2,1,0:T(2,128)(2,1)}), bf16[32,2,3584]{2,1,0:T(2,128)(2,1)}, u32[]{:S(2)}, u32[]{:S(2)}) async-start(bf16[32,2,3584]{2,1,0:T(2,128)(2,1)} %broadcast_in_dim.30), calls=%async_computation | async-start | bytes 917504 | tf_op jit(solution)/shard_map/all_to_all | solution.py:300
  14.4 4.5 %copy-start.3 = (bf16[1,2,3584]{2,1,0:T(2,128)(2,1)S(1)}, bf16[1,2,3584]{2,1,0:T(2,128)(2,1)}, u32[]{:S(2)}) copy-start(bf16[1,2,3584]{2,1,0:T(2,128)(2,1)} %param.13) | copy-start | bytes 43012
  14.5 5.6 %copy-start.2 = (s32[1,128,128]{2,1,0:T(8,128)S(1)}, s32[1,128,128]{2,1,0:T(8,128)}, u32[]{:S(2)}) copy-start(s32[1,128,128]{2,1,0:T(8,128)} %param.10) | copy-start | bytes 196612
  18.0 17.2 %collective-permute-start.2 = (bf16[4,128,1792]{2,1,0:T(8,128)(2,1)}, bf16[4,128,1792]{2,1,0:T(8,128)(2,1)}, u32[]{:S(2)}, u32[]{:S(2)}) collective-permute-start(bf16[4,128,1792]{2,1,0:T(8,128)(2,1)} %get-tuple-element.26), channel_id=1, source_target_pairs={{0,1},{1,0},{2,3},{3,2},{4,5},{5,4},{6,7},{7,6},{8,9},{9,8},{10,11... | collective-permute-start | bytes 5505032 | tf_op jit(solution)/shard_map/ppermute | solution.py:304
  19.0 15.3 %collective-permute-start.3 = (bf16[2,1792]{1,0:T(2,128)(2,1)S(1)}, bf16[2,1792]{1,0:T(2,128)(2,1)S(1)}, u32[]{:S(2)}, u32[]{:S(2)}) collective-permute-start(bf16[2,1792]{1,0:T(2,128)(2,1)S(1)} %dynamic-slice_bitcast_fusion.2), channel_id=1, source_target_pairs={{0,1},{1,0},{2,3},{3,2},{4,5},{5,4},{6,7},{7,6},{8,9},{9,8},{10,11... | collective-permute-start | bytes 21512 | tf_op jit(solution)/shard_map/ppermute | solution.py:307
  28.5 5.3 %copy-start.4 = (f32[1,128]{1,0:T(1,128)S(1)}, f32[1,128]{1,0:T(1,128)}, u32[]{:S(2)}) copy-start(f32[1,128]{1,0:T(1,128)} %param.9) | copy-start | bytes 1540
  28.5 5.0 %collective-permute-start = (bf16[64,3584]{1,0:T(8,128)(2,1)S(1)}, bf16[64,3584]{1,0:T(8,128)(2,1)S(1)}, u32[]{:S(2)}, u32[]{:S(2)}) collective-permute-start(bf16[64,3584]{1,0:T(8,128)(2,1)S(1)} %reshape.50.same), channel_id=1, source_target_pairs={{0,1},{1,0},{2,3},{3,2},{4,5},{5,4},{6,7},{7,6},{8,9},{9,8},{10,11... | collective-permute-start | bytes 1376264 | tf_op jit(solution)/shard_map/ppermute | solution.py:322
  33.9 1.3 %collective-permute-start.1 = (bf16[128,128]{1,0:T(8,128)(2,1)S(1)}, bf16[128,128]{1,0:T(8,128)(2,1)S(1)}, u32[]{:S(2)}, u32[]{:S(2)}) collective-permute-start(bf16[128,128]{1,0:T(8,128)(2,1)S(1)} %fusion.5.feats), channel_id=1, source_target_pairs={{0,1},{1,0},{2,3},{3,2},{4,5},{5,4},{6,7},{7,6},{8,9},{9,8},{10,11... | collective-permute-start | bytes 98312 | tf_op jit(solution)/shard_map/ppermute | solution.py:327
  91.6 30.1 %copy-start.1 = (bf16[1,4,128,3584]{3,2,1,0:T(8,128)(2,1)S(1)}, bf16[1,4,128,3584]{3,2,1,0:T(8,128)(2,1)}, u32[]{:S(2)}) copy-start(bf16[1,4,128,3584]{3,2,1,0:T(8,128)(2,1)} %param.11) | copy-start | bytes 11010052
  117.2 7.9 %collective-permute-start.4 = (bf16[4,16,2,8,896]{4,3,2,1,0:T(8,128)(2,1)S(1)}, bf16[4,16,2,8,896]{4,3,2,1,0:T(8,128)(2,1)S(1)}, u32[]{:S(2)}, u32[]{:S(2)}) collective-permute-start(bf16[4,16,2,8,896]{4,3,2,1,0:T(8,128)(2,1)S(1)} %bitcast.33), channel_id=1, source_target_pairs={{0,1},{1,0},{2,3},{3,2},{4,5},{5,4},{6,7},{7,6},{8,9},{9,8},{10,11... | collective-permute-start | bytes 5505032 | tf_op jit(solution)/shard_map/ppermute | solution.py:338

commit v4 on v3

--- a/solution.py
+++ b/solution.py
@@ -40,56 +40,35 @@
     return source.at[:, :, pl.ds(pl.multiple_of(side * half, half), half)]
 
 
-def recon_kernel(layer, feats, feats_other, mine, got, placed, out, held, out_held, mine_sems, got_sems, out_sems):
-    layers, rows, _ = out_held.shape
-    latents = feats.shape[1]
-    loads = []
-    for target in range(layers):
-        for which, (source, sems) in enumerate(((mine, mine_sems), (got, got_sems))):
-            place = held.at[target, pl.ds(which * latents, latents)]
-            loads.append(pltpu.make_async_copy(source.at[target], place, sems.at[target]))
-            loads[-1].start()
-    leaving = [pltpu.make_async_copy(out_held.at[t], out.at[t], out_sems.at[t]) for t in range(layers)]
-    both = jnp.concatenate([feats[...], swap_halves(feats_other[...])], axis=1)
-    for target in range(layers):
-        loads[2 * target].wait()
-        loads[2 * target + 1].wait()
+def recon_kernel(layer, feats, feats_other, mine, got, placed, out):
+    theirs = swap_halves(feats_other[...])
+    for target in range(out.shape[0]):
 
         @pl.when(target < layer[0])
         def _():
-            out_held[target] = jnp.zeros(out_held.shape[1:], BF16)
-
-        @pl.when(target > layer[0])
-        def _():
-            out_held[target] = jnp.dot(both, held[target], preferred_element_type=F32).astype(BF16)
-
-        @pl.when(target == layer[0])
-        def _():
-            total = jnp.dot(both, held[target], preferred_element_type=F32)
-            out_held[target] = (total - placed[...].astype(F32)).astype(BF16)
-
-        leaving[target].start()
-    for copy in leaving:
-        copy.wait()
+            out[target] = jnp.zeros(out.shape[1:], BF16)
+
+        @pl.when(target >= layer[0])
+        def _():
+            total = jnp.dot(feats[...], mine[target], preferred_element_type=F32) + jnp.dot(
+                theirs, got[target], preferred_element_type=F32
+            )
+            out[target] = total.astype(BF16)
+
+            @pl.when(target == layer[0])
+            def _():
+                out[target] = (total - placed[...].astype(F32)).astype(BF16)
 
 
 def recon_partials(layer, feats, feats_other, mine, got, placed):
     layers, latents, half = got.shape
     rows = feats.shape[0]
-    sems = pltpu.SemaphoreType.DMA((layers,))
     return pl.pallas_call(
         recon_kernel,
-        in_specs=[SMEM, VMEM, VMEM, ANY, ANY, VMEM],
-        out_specs=ANY,
+        in_specs=[SMEM, VMEM, VMEM, VMEM, VMEM, VMEM],
+        out_specs=VMEM,
         out_shape=jax.ShapeDtypeStruct((layers, rows, half), BF16),
-        scratch_shapes=[
-            pltpu.VMEM((layers, 2 * latents, half), BF16),
-            pltpu.VMEM((layers, rows, half), BF16),
-            sems,
-            sems,
-            sems,
-        ],
-        compiler_params=params(14),
+        compiler_params=params(10),
         cost_estimate=cost(4 * layers * rows * latents * half, 6 * layers * rows * half),
         name="recon_partials",
     )(layer, feats, feats_other, mine, got, placed)
@@ -129,34 +108,30 @@
     def tile(target, part):
         return err_of(target)[:, part].reshape(rows, quarter)
 
-    for target in range(layers):
-        err_of(target, wait=True)
-
-        @pl.when(target < layer)
-        def _():
-            held[target] = jnp.zeros(held.shape[1:], BF16)
-
-        @pl.when(target >= layer)
-        def _():
-            for part in range(2):
-                held[target, :, part * quarter : (part + 1) * quarter] = lax.dot_general(
-                    feats, tile(target, part), OVER_ROWS, preferred_element_type=F32
-                ).astype(BF16)
-
-        leaving[target].start()
     total[...] = jnp.zeros_like(total)
     for target in range(layers):
         decoder_of(target, wait=True)
 
+        @pl.when(target < layer)
+        def _():
+            held[target] = jnp.zeros(held.shape[1:], BF16)
+
         @pl.when(target >= layer)
         def _():
             for part in range(2):
+                lanes_of_part = slice(part * quarter, (part + 1) * quarter)
+                block = tile(target, part)
+                held[target, :, lanes_of_part] = lax.dot_general(
+                    feats, block, OVER_ROWS, preferred_element_type=F32
+                ).astype(BF16)
                 total[...] += lax.dot_general(
-                    tile(target, part),
-                    decoder_of(target)[:, part * quarter : (part + 1) * quarter],
+                    block,
+                    decoder_of(target)[:, lanes_of_part],
                     (((1,), (1,)), ((), ())),
                     preferred_element_type=F32,
                 )
+
+        leaving[target].start()
 
         @pl.when(target == layer)
         def _():
@@ -296,8 +271,11 @@
     chips = rows // (2 * held)
     scale = rows ** (-0.5)
 
-    copies = jnp.broadcast_to(acts[0][None], (chips, held, width))
-    same = lax.all_to_all(copies, ("x", "z"), 0, 0, tiled=True).reshape(chips * held, width)
+    tiles = width // 128
+    packed = acts[0].reshape(held, tiles, 128).transpose(1, 0, 2).reshape(tiles * held, 128)
+    copies = jnp.broadcast_to(packed[None], (chips,) + packed.shape)
+    same = lax.all_to_all(copies, ("x", "z"), 0, 0, tiled=True)
+    same = same.reshape(chips, tiles, held, 128).transpose(0, 2, 1, 3).reshape(chips * held, width)
 
     give = lax.dynamic_slice_in_dim(decoder, (1 - core) * half, half, axis=2)
     mine = lax.dynamic_slice_in_dim(decoder, core * half, half, axis=2)

time: 131 us -> 128 us (0.977)
  Pallas kernels: 13.4 us -> 11.7 us
  transfers between devices with their start and end apart: 6 -> 6, of which waited for: 4 -> 3; matrix products, arithmetic and copies ran while one was open for 5% -> 4% of each run, Pallas kernels for 3% -> 3%
where the time goes in v4:
time: 128 us
  blocking collectives  76.8 us (60%)
  starting transfers between devices  21.4 us (17%)
  Pallas kernels  11.7 us (9%)
  waiting for transfers between devices  9.19 us (7%)
  local copies, waits for them, and re-layouts  6.98 us (5%)
    all_to_all x1, blocking collectives, per_device(): lax.all_to_all(partials.reshape(16, rows // 4, half), ('y', 'x'), 0, 0, t...  29.9 us
    all_to_all x1, blocking collectives, per_device(): lax.all_to_all(jnp.broadcast_to(near[None], (16,) + near.shape), ('y', 'x...  25.6 us
    all_to_all x1, starting transfers between devices, per_device(): same = lax.all_to_all(copies, ('x', 'z'), 0, 0, tiled=True)  11.9 us
    all_to_all x1, blocking collectives, per_device(): chunks = lax.all_to_all(add_pieces(pieces), 'z', 0, 0, tiled=True)  11.1 us
    all_to_all x1, blocking collectives, per_device(): lax.all_to_all(jnp.broadcast_to(err[None], chunks.shape), 'z', 0, 0, tile...  10.2 us
    all_to_all x1, waiting for transfers between devices, per_device(): same = lax.all_to_all(copies, ('x', 'z'), 0, 0, tiled=True)  7.28 us
    pallas_call x1, Pallas kernels, other_half(): pl.pallas_call(other_half_kernel, in_specs=[SMEM, VMEM, VMEM, VMEM, VMEM,...  4.74 us
    ppermute x1, starting transfers between devices, per_device(): errs_other = lax.ppermute(errs, 'c', SWAP)  4.47 us
  transfers between devices with their start and end apart: 6, of which 3 were waited for; matrix products, arithmetic and copies ran while one was open for 4% of the time, Pallas kernels for 3%

profile of v4, /device:TPU:1, one launch (start us, length us, event | category | flops | bytes accessed | tf_op | source)
XLA Modules:
  0.0 127.7 jit_solution(12756090907089908686)
XLA Ops:
  0.6 0.0 copy-start
  0.6 0.8 reshape_squeeze.6
  1.5 0.8 broadcast_in_dim.30
  2.3 11.9 %all-to-all-start = ((bf16[32,56,128]{2,1,0:T(8,128)(2,1)}), bf16[32,56,128]{2,1,0:T(8,128)(2,1)S(1)}, u32[]{:S(2)}, u32[]{:S(2)}) async-start(bf16[32,56,128]{2,1,0:T(8,128)(2,1)} %broadcast_in_dim.30), calls=%async_computation | async-start | bytes 917504 | tf_op jit(solution)/shard_map/all_to_all | solution.py:277
  14.2 0.0 copy-start.3
  14.2 0.0 copy-start.2
  14.2 3.6 %dynamic-slice_bitcast_fusion = (bf16[4,128,1792]{2,1,0:T(8,128)(2,1)}, bf16[4,128,1792]{2,1,0:T(8,128)(2,1)S(1)}) fusion(bf16[1,4,128,3584]{3,2,1,0:T(8,128)(2,1)} %param.11, s32[]{:T(128)S(6)} %select_n.40, s32[]{:T(128)S(6)} %select_n.34), kind=kLoop, calls=%fused_computation | loop fusion | bytes 7340040 | tf_op jit(solution)/shard_map/dynamic_slice | solution.py:280
  17.8 1.0 collective-permute-start.2
  18.7 0.0 copy-done.3
  18.8 0.1 collective-permute-start.3
  18.9 0.8 dynamic-slice_reduce_fusion
  19.7 0.1 pad_add_fusion.1.layer.places
  19.8 0.0 copy-done.2
  19.8 7.3 %all-to-all-done = bf16[32,56,128]{2,1,0:T(8,128)(2,1)S(1)} async-done(((bf16[32,56,128]{2,1,0:T(8,128)(2,1)}), bf16[32,56,128]{2,1,0:T(8,128)(2,1)S(1)}, u32[]{:S(2)}, u32[]{:S(2)}) %all-to-all-start) | async-done | bytes 458784 | tf_op jit(solution)/shard_map/all_to_all | solution.py:277
  27.1 0.1 copy.19
  27.2 0.3 copy.20
  27.5 0.2 copy.27
  27.7 0.0 copy-start.4
  27.7 3.5 %collective-permute-start = (bf16[64,3584]{1,0:T(8,128)(2,1)S(1)}, bf16[64,3584]{1,0:T(8,128)(2,1)S(1)}, u32[]{:S(2)}, u32[]{:S(2)}) collective-permute-start(bf16[64,3584]{1,0:T(8,128)(2,1)S(1)} %bitcast.45), channel_id=1, source_target_pairs={{0,1},{1,0},{2,3},{3,2},{4,5},{5,4},{6,7},{7,6},{8,9},{9,8},{10,11... | collective-permute-start | bytes 1376264 | tf_op jit(solution)/shard_map/ppermute | solution.py:300
  31.3 0.0 copy-done
  31.3 0.3 fusion.2
  31.6 1.1 collective-permute-done.apart
  32.7 0.3 fusion
  33.0 0.0 copy-done.4
  33.0 0.5 collective-permute-start.1
  33.5 0.0 collective-permute-done.3
  33.5 0.8 collective-permute-done.1.feats_other
  34.3 0.0 collective-permute-done.2.got
  34.3 3.2 %recon_partials.1 = bf16[4,128,1792]{2,1,0:T(8,128)(2,1)S(1)} custom-call(s32[2]{0:T(128)S(1)} %pad_add_fusion.1.layer.places, bf16[128,128]{1,0:T(8,128)(2,1)S(1)} %fusion.5.feats, bf16[128,128]{1,0:T(8,128)(2,1)S(1)} %collective-permute-done.1.feats_other, bf16[4,128,1792]{2,1,0:T(8,128)(2,1)S(1)} %get-tuple-element.17.mine, ...), custom_call_target="tpu_custom_call" | custom-call | flops 469762048 | bytes 5505024 | tf_op jit(solution)/shard_map/recon_partials/pallas_call | solution.py:66
  37.5 29.9 %all_to_all.25.pieces = bf16[16,32,1792]{2,1,0:T(8,128)(2,1)S(1)} all-to-all(bf16[16,32,1792]{2,1,0:T(8,128)(2,1)S(1)} %bitcast.44), channel_id=1, replica_groups=mesh['y'=4,'x'=4,'z'=8,'c'=2] {'y','x'}, dimensions={0} | all-to-all | bytes 3670016 | tf_op jit(solution)/shard_map/all_to_all | solution.py:309
  67.4 0.4 add_pieces.1
  67.8 11.1 %all_to_all.26 = bf16[8,8,896]{2,1,0:T(8,128)(2,1)S(1)} all-to-all(bf16[8,8,896]{2,1,0:T(8,128)(2,1)S(1)} %add_pieces.1), channel_id=1, replica_groups=mesh['y'=4,'x'=4,'z'=8,'c'=2] {'z'}, dimensions={0} | all-to-all | bytes 229376 | tf_op jit(solution)/shard_map/all_to_all | solution.py:310
  79.0 10.2 %all_to_all.27 = bf16[8,8,896]{2,1,0:T(8,128)(2,1)S(1)} all-to-all(bf16[8,8,896]{2,1,0:T(8,128)(2,1)S(1)} %broadcast_in_dim.32), channel_id=1, replica_groups=mesh['y'=4,'x'=4,'z'=8,'c'=2] {'z'}, dimensions={0} | all-to-all | bytes 229376 | tf_op jit(solution)/shard_map/all_to_all | solution.py:313
  89.2 0.2 broadcast_in_dim.33
  89.4 0.0 copy-start.1
  89.5 25.6 %all_to_all.28 = bf16[16,8,8,896]{3,2,1,0:T(8,128)(2,1)S(1)} all-to-all(bf16[16,8,8,896]{3,2,1,0:T(8,128)(2,1)S(1)} %broadcast_in_dim.33), channel_id=1, replica_groups=mesh['y'=4,'x'=4,'z'=8,'c'=2] {'y','x'}, dimensions={0} | all-to-all | bytes 3670016 | tf_op jit(solution)/shard_map/all_to_all | solution.py:314
  115.1 4.5 %collective-permute-start.4 = (bf16[4,16,2,8,896]{4,3,2,1,0:T(8,128)(2,1)S(1)}, bf16[4,16,2,8,896]{4,3,2,1,0:T(8,128)(2,1)S(1)}, u32[]{:S(2)}, u32[]{:S(2)}) collective-permute-start(bf16[4,16,2,8,896]{4,3,2,1,0:T(8,128)(2,1)S(1)} %bitcast.42), channel_id=1, source_target_pairs={{0,1},{1,0},{2,3},{3,2},{4,5},{5,4},{6,7},{7,6},{8,9},{9,8},{10,11... | collective-permute-start | bytes 5505032 | tf_op jit(solution)/shard_map/ppermute | solution.py:316
  119.6 0.0 copy-done.1
  119.6 3.4 %own_half.1 = (bf16[4,128,3584]{2,1,0:T(8,128)(2,1)}, f32[128,128]{1,0:T(8,128)S(1)}, f32[1,1792]{1,0:T(1,128)S(1)}) custom-call(s32[2]{0:T(128)S(1)} %pad_add_fusion.1.layer.places, bf16[128,128]{1,0:T(8,128)(2,1)S(1)} %fusion.5.feats, bf16[4,16,2,8,896]{4,3,2,1,0:T(8,128)(2,1)S(1)} %bitcast.43, bf16[4,128,3584]{2,1,0:T(8,128)(2,1)S(1)} %bitcast.40), custom_call_target="tpu_custom_call" | custom-call | flops 469762048 | bytes 5505024 | tf_op jit(solution)/shard_map/own_half/pallas_call | solution.py:168
  123.0 0.0 collective-permute-done.4.errs
  123.0 4.7 %other_half.1 = (bf16[4,128,3584]{2,1,0:T(8,128)(2,1)}, f32[1,3584]{1,0:T(1,128)}, bf16[3584,128]{1,0:T(8,128)(2,1)}, f32[1,128]{1,0:T(1,128)}) custom-call(s32[2]{0:T(128)S(1)} %pad_add_fusion.1.layer.places, bf16[128,128]{1,0:T(8,128)(2,1)S(1)} %fusion.5.feats, s32[128,128]{1,0:T(8,128)S(1)} %pad_add_fusion.gate, ...), custom_call_target="tpu_custom_call", output_to_operand_aliasing={{0}: (9, {})} | custom-call | flops 704643072 | bytes 7340032 | tf_op jit(solution)/shard_map/other_half/pallas_call | solution.py:236
  (11 shorter events, 0.2 us)
Async XLA Ops:
  0.6 30.7 %copy-start = (bf16[1,3584,128]{2,1,0:T(8,128)(2,1)S(1)}, bf16[1,3584,128]{2,1,0:T(8,128)(2,1)}, u32[]{:S(2)}) copy-start(bf16[1,3584,128]{2,1,0:T(8,128)(2,1)} %param.8) | copy-start | bytes 2752516
  2.3 24.8 %all-to-all-start = ((bf16[32,56,128]{2,1,0:T(8,128)(2,1)}), bf16[32,56,128]{2,1,0:T(8,128)(2,1)S(1)}, u32[]{:S(2)}, u32[]{:S(2)}) async-start(bf16[32,56,128]{2,1,0:T(8,128)(2,1)} %broadcast_in_dim.30), calls=%async_computation | async-start | bytes 917504 | tf_op jit(solution)/shard_map/all_to_all | solution.py:277
  14.2 4.5 %copy-start.3 = (bf16[1,2,3584]{2,1,0:T(2,128)(2,1)S(1)}, bf16[1,2,3584]{2,1,0:T(2,128)(2,1)}, u32[]{:S(2)}) copy-start(bf16[1,2,3584]{2,1,0:T(2,128)(2,1)} %param.13) | copy-start | bytes 43012
  14.2 5.6 %copy-start.2 = (s32[1,128,128]{2,1,0:T(8,128)S(1)}, s32[1,128,128]{2,1,0:T(8,128)}, u32[]{:S(2)}) copy-start(s32[1,128,128]{2,1,0:T(8,128)} %param.10) | copy-start | bytes 196612
  17.8 16.6 %collective-permute-start.2 = (bf16[4,128,1792]{2,1,0:T(8,128)(2,1)}, bf16[4,128,1792]{2,1,0:T(8,128)(2,1)}, u32[]{:S(2)}, u32[]{:S(2)}) collective-permute-start(bf16[4,128,1792]{2,1,0:T(8,128)(2,1)} %get-tuple-element.26), channel_id=1, source_target_pairs={{0,1},{1,0},{2,3},{3,2},{4,5},{5,4},{6,7},{7,6},{8,9},{9,8},{10,11... | collective-permute-start | bytes 5505032 | tf_op jit(solution)/shard_map/ppermute | solution.py:282
  18.8 14.7 %collective-permute-start.3 = (bf16[2,1792]{1,0:T(2,128)(2,1)S(1)}, bf16[2,1792]{1,0:T(2,128)(2,1)S(1)}, u32[]{:S(2)}, u32[]{:S(2)}) collective-permute-start(bf16[2,1792]{1,0:T(2,128)(2,1)S(1)} %dynamic-slice_bitcast_fusion.2), channel_id=1, source_target_pairs={{0,1},{1,0},{2,3},{3,2},{4,5},{5,4},{6,7},{7,6},{8,9},{9,8},{10,11... | collective-permute-start | bytes 21512 | tf_op jit(solution)/shard_map/ppermute | solution.py:285
  27.7 5.3 %copy-start.4 = (f32[1,128]{1,0:T(1,128)S(1)}, f32[1,128]{1,0:T(1,128)}, u32[]{:S(2)}) copy-start(f32[1,128]{1,0:T(1,128)} %param.9) | copy-start | bytes 1540
  27.7 5.0 %collective-permute-start = (bf16[64,3584]{1,0:T(8,128)(2,1)S(1)}, bf16[64,3584]{1,0:T(8,128)(2,1)S(1)}, u32[]{:S(2)}, u32[]{:S(2)}) collective-permute-start(bf16[64,3584]{1,0:T(8,128)(2,1)S(1)} %bitcast.45), channel_id=1, source_target_pairs={{0,1},{1,0},{2,3},{3,2},{4,5},{5,4},{6,7},{7,6},{8,9},{9,8},{10,11... | collective-permute-start | bytes 1376264 | tf_op jit(solution)/shard_map/ppermute | solution.py:300
  33.0 1.3 %collective-permute-start.1 = (bf16[128,128]{1,0:T(8,128)(2,1)S(1)}, bf16[128,128]{1,0:T(8,128)(2,1)S(1)}, u32[]{:S(2)}, u32[]{:S(2)}) collective-permute-start(bf16[128,128]{1,0:T(8,128)(2,1)S(1)} %fusion.5.feats), channel_id=1, source_target_pairs={{0,1},{1,0},{2,3},{3,2},{4,5},{5,4},{6,7},{7,6},{8,9},{9,8},{10,11... | collective-permute-start | bytes 98312 | tf_op jit(solution)/shard_map/ppermute | solution.py:305
  89.4 30.1 %copy-start.1 = (bf16[1,4,128,3584]{3,2,1,0:T(8,128)(2,1)S(1)}, bf16[1,4,128,3584]{3,2,1,0:T(8,128)(2,1)}, u32[]{:S(2)}) copy-start(bf16[1,4,128,3584]{3,2,1,0:T(8,128)(2,1)} %param.11) | copy-start | bytes 11010052
  115.1 7.9 %collective-permute-start.4 = (bf16[4,16,2,8,896]{4,3,2,1,0:T(8,128)(2,1)S(1)}, bf16[4,16,2,8,896]{4,3,2,1,0:T(8,128)(2,1)S(1)}, u32[]{:S(2)}, u32[]{:S(2)}) collective-permute-start(bf16[4,16,2,8,896]{4,3,2,1,0:T(8,128)(2,1)S(1)} %bitcast.42), channel_id=1, source_target_pairs={{0,1},{1,0},{2,3},{3,2},{4,5},{5,4},{6,7},{7,6},{8,9},{9,8},{10,11... | collective-permute-start | bytes 5505032 | tf_op jit(solution)/shard_map/ppermute | solution.py:316

commit v5 on v4

--- a/solution.py
+++ b/solution.py
@@ -35,13 +35,32 @@
     return copies
 
 
+def copies_kernel(acts, out):
+    tiles = [acts[0, :, start : start + 128].astype(F32) for start in range(0, acts.shape[2], 128)]
+    packed = jnp.concatenate(tiles, axis=0).astype(BF16)
+    out[...] = jnp.broadcast_to(packed[None], out.shape)
+
+
+def copies_of_rows(acts, chips):
+    _, held, width = acts.shape
+    return pl.pallas_call(
+        copies_kernel,
+        in_specs=[VMEM],
+        out_specs=VMEM,
+        out_shape=jax.ShapeDtypeStruct((chips, held * width // 128, 128), BF16),
+        compiler_params=params(4),
+        cost_estimate=cost(0, 2 * chips * held * width),
+        name="copies_of_rows",
+    )(acts)
+
+
 def half_of(source, side, held):
     half = held.shape[2]
     return source.at[:, :, pl.ds(pl.multiple_of(side * half, half), half)]
 
 
 def recon_kernel(layer, feats, feats_other, mine, got, placed, out):
-    theirs = swap_halves(feats_other[...])
+    both = jnp.concatenate([feats[...], swap_halves(feats_other[...])], axis=1)
     for target in range(out.shape[0]):
 
         @pl.when(target < layer[0])
@@ -50,9 +69,8 @@
 
         @pl.when(target >= layer[0])
         def _():
-            total = jnp.dot(feats[...], mine[target], preferred_element_type=F32) + jnp.dot(
-                theirs, got[target], preferred_element_type=F32
-            )
+            decoders = jnp.concatenate([mine[target], got[target]], axis=0)
+            total = jnp.dot(both, decoders, preferred_element_type=F32)
             out[target] = total.astype(BF16)
 
             @pl.when(target == layer[0])
@@ -272,8 +290,7 @@
     scale = rows ** (-0.5)
 
     tiles = width // 128
-    packed = acts[0].reshape(held, tiles, 128).transpose(1, 0, 2).reshape(tiles * held, 128)
-    copies = jnp.broadcast_to(packed[None], (chips,) + packed.shape)
+    copies = copies_of_rows(acts, chips)
     same = lax.all_to_all(copies, ("x", "z"), 0, 0, tiled=True)
     same = same.reshape(chips, tiles, held, 128).transpose(0, 2, 1, 3).reshape(chips * held, width)
 

time: 128 us -> 128 us (level)
  no operation moved by 1% of the time
where the time goes in v5:
time: 128 us; the launch traced here: 127 us
  blocking collectives  77 us (60%)
  starting transfers between devices  21.4 us (17%)
  Pallas kernels  12.2 us (10%)
  waiting for transfers between devices  9.19 us (7%)
  local copies, waits for them, and re-layouts  5.85 us (5%)
    all_to_all x1, blocking collectives, per_device(): lax.all_to_all(partials.reshape(16, rows // 4, half), ('y', 'x'), 0, 0, t...  30.1 us
    all_to_all x1, blocking collectives, per_device(): lax.all_to_all(jnp.broadcast_to(near[None], (16,) + near.shape), ('y', 'x...  25.6 us
    all_to_all x1, starting transfers between devices, per_device(): same = lax.all_to_all(copies, ('x', 'z'), 0, 0, tiled=True)  11.9 us
    all_to_all x1, blocking collectives, per_device(): chunks = lax.all_to_all(add_pieces(pieces), 'z', 0, 0, tiled=True)  11.1 us
    all_to_all x1, blocking collectives, per_device(): lax.all_to_all(jnp.broadcast_to(err[None], chunks.shape), 'z', 0, 0, tile...  10.2 us
    all_to_all x1, waiting for transfers between devices, per_device(): same = lax.all_to_all(copies, ('x', 'z'), 0, 0, tiled=True)  7.28 us
    pallas_call x1, Pallas kernels, other_half(): pl.pallas_call(other_half_kernel, in_specs=[SMEM, VMEM, VMEM, VMEM, VMEM,...  4.75 us
    ppermute x1, starting transfers between devices, per_device(): errs_other = lax.ppermute(errs, 'c', SWAP)  4.47 us
  transfers between devices with their start and end apart: 6, of which 3 were waited for; matrix products, arithmetic and copies ran while one was open for 4% of the time, Pallas kernels for 3%

profile of v5, /device:TPU:1, one launch (start us, length us, event | category | flops | bytes accessed | tf_op | source)
XLA Modules:
  0.0 127.2 jit_solution(12142607015263296783)
XLA Ops:
  0.6 0.0 copy-start
  0.6 0.0 copy-start.2
  0.7 0.8 copy-done.2
  1.4 0.8 copies_of_rows.1
  2.2 11.9 %all-to-all-start = ((bf16[32,56,128]{2,1,0:T(8,128)(2,1)}), bf16[32,56,128]{2,1,0:T(8,128)(2,1)S(1)}, u32[]{:S(2)}, u32[]{:S(2)}) async-start(bf16[32,56,128]{2,1,0:T(8,128)(2,1)} %copies_of_rows.1), calls=%async_computation | async-start | bytes 917504 | tf_op jit(solution)/shard_map/all_to_all | solution.py:294
  14.1 0.0 copy-start.4
  14.1 0.0 copy-start.3
  14.2 3.6 %dynamic-slice_bitcast_fusion = (bf16[4,128,1792]{2,1,0:T(8,128)(2,1)}, bf16[4,128,1792]{2,1,0:T(8,128)(2,1)S(1)}) fusion(bf16[1,4,128,3584]{3,2,1,0:T(8,128)(2,1)} %param.11, s32[]{:T(128)S(6)} %select_n.40, s32[]{:T(128)S(6)} %select_n.34), kind=kLoop, calls=%fused_computation | loop fusion | bytes 7340040 | tf_op jit(solution)/shard_map/dynamic_slice | solution.py:297
  17.7 1.0 collective-permute-start.2
  18.7 0.0 copy-done.4
  18.7 0.1 collective-permute-start.3
  18.8 0.8 dynamic-slice_reduce_fusion
  19.6 0.1 pad_add_fusion.1.layer.places
  19.7 0.0 copy-done.3
  19.7 7.3 %all-to-all-done = bf16[32,56,128]{2,1,0:T(8,128)(2,1)S(1)} async-done(((bf16[32,56,128]{2,1,0:T(8,128)(2,1)}), bf16[32,56,128]{2,1,0:T(8,128)(2,1)S(1)}, u32[]{:S(2)}, u32[]{:S(2)}) %all-to-all-start) | async-done | bytes 458784 | tf_op jit(solution)/shard_map/all_to_all | solution.py:294
  27.0 0.1 copy.15
  27.1 0.2 copy.22
  27.3 0.0 copy-start.5
  27.4 3.5 %collective-permute-start = (bf16[64,3584]{1,0:T(8,128)(2,1)S(1)}, bf16[64,3584]{1,0:T(8,128)(2,1)S(1)}, u32[]{:S(2)}, u32[]{:S(2)}) collective-permute-start(bf16[64,3584]{1,0:T(8,128)(2,1)S(1)} %bitcast.42), channel_id=1, source_target_pairs={{0,1},{1,0},{2,3},{3,2},{4,5},{5,4},{6,7},{7,6},{8,9},{9,8},{10,11... | collective-permute-start | bytes 1376264 | tf_op jit(solution)/shard_map/ppermute | solution.py:317
  31.0 0.0 copy-done
  31.0 0.3 fusion.2
  31.3 1.1 collective-permute-done.apart
  32.3 0.3 fusion
  32.6 0.0 copy-done.5
  32.7 0.5 collective-permute-start.1
  33.1 0.0 collective-permute-done.3
  33.2 0.8 collective-permute-done.1.feats_other
  34.0 0.0 collective-permute-done.2.got
  34.0 2.8 %recon_partials.1 = bf16[4,128,1792]{2,1,0:T(8,128)(2,1)S(1)} custom-call(s32[2]{0:T(128)S(1)} %pad_add_fusion.1.layer.places, bf16[128,128]{1,0:T(8,128)(2,1)S(1)} %fusion.5.feats, bf16[128,128]{1,0:T(8,128)(2,1)S(1)} %collective-permute-done.1.feats_other, bf16[4,128,1792]{2,1,0:T(8,128)(2,1)S(1)} %get-tuple-element.17.mine, ...), custom_call_target="tpu_custom_call" | custom-call | flops 469762048 | bytes 5505024 | tf_op jit(solution)/shard_map/recon_partials/pallas_call | solution.py:84
  36.8 30.1 %all_to_all.25.pieces = bf16[16,32,1792]{2,1,0:T(8,128)(2,1)S(1)} all-to-all(bf16[16,32,1792]{2,1,0:T(8,128)(2,1)S(1)} %bitcast.41), channel_id=1, replica_groups=mesh['y'=4,'x'=4,'z'=8,'c'=2] {'y','x'}, dimensions={0} | all-to-all | bytes 3670016 | tf_op jit(solution)/shard_map/all_to_all | solution.py:326
  66.9 0.4 add_pieces.1
  67.3 11.1 %all_to_all.26 = bf16[8,8,896]{2,1,0:T(8,128)(2,1)S(1)} all-to-all(bf16[8,8,896]{2,1,0:T(8,128)(2,1)S(1)} %add_pieces.1), channel_id=1, replica_groups=mesh['y'=4,'x'=4,'z'=8,'c'=2] {'z'}, dimensions={0} | all-to-all | bytes 229376 | tf_op jit(solution)/shard_map/all_to_all | solution.py:327
  78.5 10.2 %all_to_all.27 = bf16[8,8,896]{2,1,0:T(8,128)(2,1)S(1)} all-to-all(bf16[8,8,896]{2,1,0:T(8,128)(2,1)S(1)} %broadcast_in_dim.11), channel_id=1, replica_groups=mesh['y'=4,'x'=4,'z'=8,'c'=2] {'z'}, dimensions={0} | all-to-all | bytes 229376 | tf_op jit(solution)/shard_map/all_to_all | solution.py:330
  88.7 0.2 broadcast_in_dim.24
  88.9 0.0 copy-start.1
  88.9 25.6 %all_to_all.28 = bf16[16,8,8,896]{3,2,1,0:T(8,128)(2,1)S(1)} all-to-all(bf16[16,8,8,896]{3,2,1,0:T(8,128)(2,1)S(1)} %broadcast_in_dim.24), channel_id=1, replica_groups=mesh['y'=4,'x'=4,'z'=8,'c'=2] {'y','x'}, dimensions={0} | all-to-all | bytes 3670016 | tf_op jit(solution)/shard_map/all_to_all | solution.py:331
  114.6 4.5 %collective-permute-start.4 = (bf16[4,16,2,8,896]{4,3,2,1,0:T(8,128)(2,1)S(1)}, bf16[4,16,2,8,896]{4,3,2,1,0:T(8,128)(2,1)S(1)}, u32[]{:S(2)}, u32[]{:S(2)}) collective-permute-start(bf16[4,16,2,8,896]{4,3,2,1,0:T(8,128)(2,1)S(1)} %bitcast.39), channel_id=1, source_target_pairs={{0,1},{1,0},{2,3},{3,2},{4,5},{5,4},{6,7},{7,6},{8,9},{9,8},{10,11... | collective-permute-start | bytes 5505032 | tf_op jit(solution)/shard_map/ppermute | solution.py:333
  119.0 0.0 copy-done.1
  119.0 3.4 %own_half.1 = (bf16[4,128,3584]{2,1,0:T(8,128)(2,1)}, f32[128,128]{1,0:T(8,128)S(1)}, f32[1,1792]{1,0:T(1,128)S(1)}) custom-call(s32[2]{0:T(128)S(1)} %pad_add_fusion.1.layer.places, bf16[128,128]{1,0:T(8,128)(2,1)S(1)} %fusion.5.feats, bf16[4,16,2,8,896]{4,3,2,1,0:T(8,128)(2,1)S(1)} %bitcast.40, bf16[4,128,3584]{2,1,0:T(8,128)(2,1)S(1)} %bitcast.37), custom_call_target="tpu_custom_call" | custom-call | flops 469762048 | bytes 5505024 | tf_op jit(solution)/shard_map/own_half/pallas_call | solution.py:186
  122.4 0.0 collective-permute-done.4.errs
  122.5 4.7 %other_half.1 = (bf16[4,128,3584]{2,1,0:T(8,128)(2,1)}, f32[1,3584]{1,0:T(1,128)}, bf16[3584,128]{1,0:T(8,128)(2,1)}, f32[1,128]{1,0:T(1,128)}) custom-call(s32[2]{0:T(128)S(1)} %pad_add_fusion.1.layer.places, bf16[128,128]{1,0:T(8,128)(2,1)S(1)} %fusion.5.feats, s32[128,128]{1,0:T(8,128)S(1)} %pad_add_fusion.gate, ...), custom_call_target="tpu_custom_call", output_to_operand_aliasing={{0}: (9, {})} | custom-call | flops 704643072 | bytes 7340032 | tf_op jit(solution)/shard_map/other_half/pallas_call | solution.py:254
  (10 shorter events, 0.2 us)
Async XLA Ops:
  0.6 30.3 %copy-start = (bf16[1,3584,128]{2,1,0:T(8,128)(2,1)S(1)}, bf16[1,3584,128]{2,1,0:T(8,128)(2,1)}, u32[]{:S(2)}) copy-start(bf16[1,3584,128]{2,1,0:T(8,128)(2,1)} %param.8) | copy-start | bytes 2752516
  0.6 0.8 copy-start.2
  2.2 24.8 %all-to-all-start = ((bf16[32,56,128]{2,1,0:T(8,128)(2,1)}), bf16[32,56,128]{2,1,0:T(8,128)(2,1)S(1)}, u32[]{:S(2)}, u32[]{:S(2)}) async-start(bf16[32,56,128]{2,1,0:T(8,128)(2,1)} %copies_of_rows.1), calls=%async_computation | async-start | bytes 917504 | tf_op jit(solution)/shard_map/all_to_all | solution.py:294
  14.1 4.5 %copy-start.4 = (bf16[1,2,3584]{2,1,0:T(2,128)(2,1)S(1)}, bf16[1,2,3584]{2,1,0:T(2,128)(2,1)}, u32[]{:S(2)}) copy-start(bf16[1,2,3584]{2,1,0:T(2,128)(2,1)} %param.13) | copy-start | bytes 43012
  14.1 5.6 %copy-start.3 = (s32[1,128,128]{2,1,0:T(8,128)S(1)}, s32[1,128,128]{2,1,0:T(8,128)}, u32[]{:S(2)}) copy-start(s32[1,128,128]{2,1,0:T(8,128)} %param.10) | copy-start | bytes 196612
  17.7 16.3 %collective-permute-start.2 = (bf16[4,128,1792]{2,1,0:T(8,128)(2,1)}, bf16[4,128,1792]{2,1,0:T(8,128)(2,1)}, u32[]{:S(2)}, u32[]{:S(2)}) collective-permute-start(bf16[4,128,1792]{2,1,0:T(8,128)(2,1)} %get-tuple-element.26), channel_id=1, source_target_pairs={{0,1},{1,0},{2,3},{3,2},{4,5},{5,4},{6,7},{7,6},{8,9},{9,8},{10,11... | collective-permute-start | bytes 5505032 | tf_op jit(solution)/shard_map/ppermute | solution.py:299
  18.7 14.4 %collective-permute-start.3 = (bf16[2,1792]{1,0:T(2,128)(2,1)S(1)}, bf16[2,1792]{1,0:T(2,128)(2,1)S(1)}, u32[]{:S(2)}, u32[]{:S(2)}) collective-permute-start(bf16[2,1792]{1,0:T(2,128)(2,1)S(1)} %dynamic-slice_bitcast_fusion.2), channel_id=1, source_target_pairs={{0,1},{1,0},{2,3},{3,2},{4,5},{5,4},{6,7},{7,6},{8,9},{9,8},{10,11... | collective-permute-start | bytes 21512 | tf_op jit(solution)/shard_map/ppermute | solution.py:302
  27.3 5.3 %copy-start.5 = (f32[1,128]{1,0:T(1,128)S(1)}, f32[1,128]{1,0:T(1,128)}, u32[]{:S(2)}) copy-start(f32[1,128]{1,0:T(1,128)} %param.9) | copy-start | bytes 1540
  27.4 5.0 %collective-permute-start = (bf16[64,3584]{1,0:T(8,128)(2,1)S(1)}, bf16[64,3584]{1,0:T(8,128)(2,1)S(1)}, u32[]{:S(2)}, u32[]{:S(2)}) collective-permute-start(bf16[64,3584]{1,0:T(8,128)(2,1)S(1)} %bitcast.42), channel_id=1, source_target_pairs={{0,1},{1,0},{2,3},{3,2},{4,5},{5,4},{6,7},{7,6},{8,9},{9,8},{10,11... | collective-permute-start | bytes 1376264 | tf_op jit(solution)/shard_map/ppermute | solution.py:317
  32.7 1.3 %collective-permute-start.1 = (bf16[128,128]{1,0:T(8,128)(2,1)S(1)}, bf16[128,128]{1,0:T(8,128)(2,1)S(1)}, u32[]{:S(2)}, u32[]{:S(2)}) collective-permute-start(bf16[128,128]{1,0:T(8,128)(2,1)S(1)} %fusion.5.feats), channel_id=1, source_target_pairs={{0,1},{1,0},{2,3},{3,2},{4,5},{5,4},{6,7},{7,6},{8,9},{9,8},{10,11... | collective-permute-start | bytes 98312 | tf_op jit(solution)/shard_map/ppermute | solution.py:322
  88.9 30.1 %copy-start.1 = (bf16[1,4,128,3584]{3,2,1,0:T(8,128)(2,1)S(1)}, bf16[1,4,128,3584]{3,2,1,0:T(8,128)(2,1)}, u32[]{:S(2)}) copy-start(bf16[1,4,128,3584]{3,2,1,0:T(8,128)(2,1)} %param.11) | copy-start | bytes 11010052
  114.6 7.9 %collective-permute-start.4 = (bf16[4,16,2,8,896]{4,3,2,1,0:T(8,128)(2,1)S(1)}, bf16[4,16,2,8,896]{4,3,2,1,0:T(8,128)(2,1)S(1)}, u32[]{:S(2)}, u32[]{:S(2)}) collective-permute-start(bf16[4,16,2,8,896]{4,3,2,1,0:T(8,128)(2,1)S(1)} %bitcast.39), channel_id=1, source_target_pairs={{0,1},{1,0},{2,3},{3,2},{4,5},{5,4},{6,7},{7,6},{8,9},{9,8},{10,11... | collective-permute-start | bytes 5505032 | tf_op jit(solution)/shard_map/ppermute | solution.py:333

commit v6 on v5

--- a/solution.py
+++ b/solution.py
@@ -136,18 +136,11 @@
 
         @pl.when(target >= layer)
         def _():
-            for part in range(2):
-                lanes_of_part = slice(part * quarter, (part + 1) * quarter)
-                block = tile(target, part)
-                held[target, :, lanes_of_part] = lax.dot_general(
-                    feats, block, OVER_ROWS, preferred_element_type=F32
-                ).astype(BF16)
-                total[...] += lax.dot_general(
-                    block,
-                    decoder_of(target)[:, lanes_of_part],
-                    (((1,), (1,)), ((), ())),
-                    preferred_element_type=F32,
-                )
+            block = jnp.concatenate([tile(target, part) for part in range(2)], axis=1)
+            held[target] = lax.dot_general(feats, block, OVER_ROWS, preferred_element_type=F32).astype(BF16)
+            total[...] += lax.dot_general(
+                block, decoder_of(target)[...], (((1,), (1,)), ((), ())), preferred_element_type=F32
+            )
 
         leaving[target].start()
 

time: 128 us -> 128 us (level)
  transfers between devices with their start and end apart: 6 -> 6, of which waited for: 3 -> 4; matrix products, arithmetic and copies ran while one was open for 4% -> 4% of each run, Pallas kernels for 3% -> 3%
where the time goes in v6:
time: 128 us; the launch traced here: 127 us
  blocking collectives  77 us (60%)
  starting transfers between devices  21.4 us (17%)
  Pallas kernels  12 us (9%)
  waiting for transfers between devices  9.25 us (7%)
  local copies, waits for them, and re-layouts  5.85 us (5%)
    all_to_all x1, blocking collectives, per_device(): lax.all_to_all(partials.reshape(16, rows // 4, half), ('y', 'x'), 0, 0, t...  30.1 us
    all_to_all x1, blocking collectives, per_device(): lax.all_to_all(jnp.broadcast_to(near[None], (16,) + near.shape), ('y', 'x...  25.6 us
    all_to_all x1, starting transfers between devices, per_device(): same = lax.all_to_all(copies, ('x', 'z'), 0, 0, tiled=True)  11.9 us
    all_to_all x1, blocking collectives, per_device(): chunks = lax.all_to_all(add_pieces(pieces), 'z', 0, 0, tiled=True)  11.1 us
    all_to_all x1, blocking collectives, per_device(): lax.all_to_all(jnp.broadcast_to(err[None], chunks.shape), 'z', 0, 0, tile...  10.2 us
    all_to_all x1, waiting for transfers between devices, per_device(): same = lax.all_to_all(copies, ('x', 'z'), 0, 0, tiled=True)  7.28 us
    pallas_call x1, Pallas kernels, other_half(): pl.pallas_call(other_half_kernel, in_specs=[SMEM, VMEM, VMEM, VMEM, VMEM,...  4.67 us
    ppermute x1, starting transfers between devices, per_device(): errs_other = lax.ppermute(errs, 'c', SWAP)  4.47 us
  transfers between devices with their start and end apart: 6, of which 4 were waited for; matrix products, arithmetic and copies ran while one was open for 4% of the time, Pallas kernels for 3%

profile of v6, /device:TPU:1, one launch (start us, length us, event | category | flops | bytes accessed | tf_op | source)
XLA Modules:
  0.0 127.1 jit_solution(5796582708686438263)
XLA Ops:
  0.6 0.0 copy-start
  0.6 0.0 copy-start.2
  0.7 0.8 copy-done.2
  1.4 0.8 copies_of_rows.1
  2.2 11.9 %all-to-all-start = ((bf16[32,56,128]{2,1,0:T(8,128)(2,1)}), bf16[32,56,128]{2,1,0:T(8,128)(2,1)S(1)}, u32[]{:S(2)}, u32[]{:S(2)}) async-start(bf16[32,56,128]{2,1,0:T(8,128)(2,1)} %copies_of_rows.1), calls=%async_computation | async-start | bytes 917504 | tf_op jit(solution)/shard_map/all_to_all | solution.py:287
  14.1 0.0 copy-start.4
  14.1 0.0 copy-start.3
  14.2 3.6 %dynamic-slice_bitcast_fusion = (bf16[4,128,1792]{2,1,0:T(8,128)(2,1)}, bf16[4,128,1792]{2,1,0:T(8,128)(2,1)S(1)}) fusion(bf16[1,4,128,3584]{3,2,1,0:T(8,128)(2,1)} %param.11, s32[]{:T(128)S(6)} %select_n.40, s32[]{:T(128)S(6)} %select_n.34), kind=kLoop, calls=%fused_computation | loop fusion | bytes 7340040 | tf_op jit(solution)/shard_map/dynamic_slice | solution.py:290
  17.7 1.0 collective-permute-start.2
  18.7 0.0 copy-done.4
  18.7 0.1 collective-permute-start.3
  18.8 0.8 dynamic-slice_reduce_fusion
  19.6 0.1 pad_add_fusion.1.layer.places
  19.7 0.0 copy-done.3
  19.7 7.3 %all-to-all-done = bf16[32,56,128]{2,1,0:T(8,128)(2,1)S(1)} async-done(((bf16[32,56,128]{2,1,0:T(8,128)(2,1)}), bf16[32,56,128]{2,1,0:T(8,128)(2,1)S(1)}, u32[]{:S(2)}, u32[]{:S(2)}) %all-to-all-start) | async-done | bytes 458784 | tf_op jit(solution)/shard_map/all_to_all | solution.py:287
  27.0 0.1 copy.15
  27.1 0.2 copy.22
  27.3 0.0 copy-start.5
  27.4 3.5 %collective-permute-start = (bf16[64,3584]{1,0:T(8,128)(2,1)S(1)}, bf16[64,3584]{1,0:T(8,128)(2,1)S(1)}, u32[]{:S(2)}, u32[]{:S(2)}) collective-permute-start(bf16[64,3584]{1,0:T(8,128)(2,1)S(1)} %bitcast.42), channel_id=1, source_target_pairs={{0,1},{1,0},{2,3},{3,2},{4,5},{5,4},{6,7},{7,6},{8,9},{9,8},{10,11... | collective-permute-start | bytes 1376264 | tf_op jit(solution)/shard_map/ppermute | solution.py:310
  31.0 0.0 copy-done
  31.0 0.3 fusion.2
  31.3 1.1 collective-permute-done.apart
  32.3 0.3 fusion
  32.6 0.0 copy-done.5
  32.7 0.5 collective-permute-start.1
  33.1 0.0 collective-permute-done.3
  33.2 0.8 collective-permute-done.1.feats_other
  34.0 0.0 collective-permute-done.2.got
  34.0 2.8 %recon_partials.1 = bf16[4,128,1792]{2,1,0:T(8,128)(2,1)S(1)} custom-call(s32[2]{0:T(128)S(1)} %pad_add_fusion.1.layer.places, bf16[128,128]{1,0:T(8,128)(2,1)S(1)} %fusion.5.feats, bf16[128,128]{1,0:T(8,128)(2,1)S(1)} %collective-permute-done.1.feats_other, bf16[4,128,1792]{2,1,0:T(8,128)(2,1)S(1)} %get-tuple-element.17.mine, ...), custom_call_target="tpu_custom_call" | custom-call | flops 469762048 | bytes 5505024 | tf_op jit(solution)/shard_map/recon_partials/pallas_call | solution.py:84
  36.8 30.1 %all_to_all.25.pieces = bf16[16,32,1792]{2,1,0:T(8,128)(2,1)S(1)} all-to-all(bf16[16,32,1792]{2,1,0:T(8,128)(2,1)S(1)} %bitcast.41), channel_id=1, replica_groups=mesh['y'=4,'x'=4,'z'=8,'c'=2] {'y','x'}, dimensions={0} | all-to-all | bytes 3670016 | tf_op jit(solution)/shard_map/all_to_all | solution.py:319
  66.9 0.4 add_pieces.1
  67.3 11.1 %all_to_all.26 = bf16[8,8,896]{2,1,0:T(8,128)(2,1)S(1)} all-to-all(bf16[8,8,896]{2,1,0:T(8,128)(2,1)S(1)} %add_pieces.1), channel_id=1, replica_groups=mesh['y'=4,'x'=4,'z'=8,'c'=2] {'z'}, dimensions={0} | all-to-all | bytes 229376 | tf_op jit(solution)/shard_map/all_to_all | solution.py:320
  78.5 10.2 %all_to_all.27 = bf16[8,8,896]{2,1,0:T(8,128)(2,1)S(1)} all-to-all(bf16[8,8,896]{2,1,0:T(8,128)(2,1)S(1)} %broadcast_in_dim.11), channel_id=1, replica_groups=mesh['y'=4,'x'=4,'z'=8,'c'=2] {'z'}, dimensions={0} | all-to-all | bytes 229376 | tf_op jit(solution)/shard_map/all_to_all | solution.py:323
  88.7 0.2 broadcast_in_dim.24
  88.9 0.0 copy-start.1
  88.9 25.6 %all_to_all.28 = bf16[16,8,8,896]{3,2,1,0:T(8,128)(2,1)S(1)} all-to-all(bf16[16,8,8,896]{3,2,1,0:T(8,128)(2,1)S(1)} %broadcast_in_dim.24), channel_id=1, replica_groups=mesh['y'=4,'x'=4,'z'=8,'c'=2] {'y','x'}, dimensions={0} | all-to-all | bytes 3670016 | tf_op jit(solution)/shard_map/all_to_all | solution.py:324
  114.6 4.5 %collective-permute-start.4 = (bf16[4,16,2,8,896]{4,3,2,1,0:T(8,128)(2,1)S(1)}, bf16[4,16,2,8,896]{4,3,2,1,0:T(8,128)(2,1)S(1)}, u32[]{:S(2)}, u32[]{:S(2)}) collective-permute-start(bf16[4,16,2,8,896]{4,3,2,1,0:T(8,128)(2,1)S(1)} %bitcast.39), channel_id=1, source_target_pairs={{0,1},{1,0},{2,3},{3,2},{4,5},{5,4},{6,7},{7,6},{8,9},{9,8},{10,11... | collective-permute-start | bytes 5505032 | tf_op jit(solution)/shard_map/ppermute | solution.py:326
  119.0 0.0 copy-done.1
  119.0 3.3 %own_half.1 = (bf16[4,128,3584]{2,1,0:T(8,128)(2,1)}, f32[128,128]{1,0:T(8,128)S(1)}, f32[1,1792]{1,0:T(1,128)S(1)}) custom-call(s32[2]{0:T(128)S(1)} %pad_add_fusion.1.layer.places, bf16[128,128]{1,0:T(8,128)(2,1)S(1)} %fusion.5.feats, bf16[4,16,2,8,896]{4,3,2,1,0:T(8,128)(2,1)S(1)} %bitcast.40, bf16[4,128,3584]{2,1,0:T(8,128)(2,1)S(1)} %bitcast.37), custom_call_target="tpu_custom_call" | custom-call | flops 469762048 | bytes 5505024 | tf_op jit(solution)/shard_map/own_half/pallas_call | solution.py:179
  122.4 0.1 collective-permute-done.4.errs
  122.5 4.7 %other_half.1 = (bf16[4,128,3584]{2,1,0:T(8,128)(2,1)}, f32[1,3584]{1,0:T(1,128)}, bf16[3584,128]{1,0:T(8,128)(2,1)}, f32[1,128]{1,0:T(1,128)}) custom-call(s32[2]{0:T(128)S(1)} %pad_add_fusion.1.layer.places, bf16[128,128]{1,0:T(8,128)(2,1)S(1)} %fusion.5.feats, s32[128,128]{1,0:T(8,128)S(1)} %pad_add_fusion.gate, ...), custom_call_target="tpu_custom_call", output_to_operand_aliasing={{0}: (9, {})} | custom-call | flops 704643072 | bytes 7340032 | tf_op jit(solution)/shard_map/other_half/pallas_call | solution.py:247
  (10 shorter events, 0.2 us)
Async XLA Ops:
  0.6 30.3 %copy-start = (bf16[1,3584,128]{2,1,0:T(8,128)(2,1)S(1)}, bf16[1,3584,128]{2,1,0:T(8,128)(2,1)}, u32[]{:S(2)}) copy-start(bf16[1,3584,128]{2,1,0:T(8,128)(2,1)} %param.8) | copy-start | bytes 2752516
  0.6 0.8 copy-start.2
  2.2 24.8 %all-to-all-start = ((bf16[32,56,128]{2,1,0:T(8,128)(2,1)}), bf16[32,56,128]{2,1,0:T(8,128)(2,1)S(1)}, u32[]{:S(2)}, u32[]{:S(2)}) async-start(bf16[32,56,128]{2,1,0:T(8,128)(2,1)} %copies_of_rows.1), calls=%async_computation | async-start | bytes 917504 | tf_op jit(solution)/shard_map/all_to_all | solution.py:287
  14.1 4.5 %copy-start.4 = (bf16[1,2,3584]{2,1,0:T(2,128)(2,1)S(1)}, bf16[1,2,3584]{2,1,0:T(2,128)(2,1)}, u32[]{:S(2)}) copy-start(bf16[1,2,3584]{2,1,0:T(2,128)(2,1)} %param.13) | copy-start | bytes 43012
  14.1 5.6 %copy-start.3 = (s32[1,128,128]{2,1,0:T(8,128)S(1)}, s32[1,128,128]{2,1,0:T(8,128)}, u32[]{:S(2)}) copy-start(s32[1,128,128]{2,1,0:T(8,128)} %param.10) | copy-start | bytes 196612
  17.7 16.3 %collective-permute-start.2 = (bf16[4,128,1792]{2,1,0:T(8,128)(2,1)}, bf16[4,128,1792]{2,1,0:T(8,128)(2,1)}, u32[]{:S(2)}, u32[]{:S(2)}) collective-permute-start(bf16[4,128,1792]{2,1,0:T(8,128)(2,1)} %get-tuple-element.26), channel_id=1, source_target_pairs={{0,1},{1,0},{2,3},{3,2},{4,5},{5,4},{6,7},{7,6},{8,9},{9,8},{10,11... | collective-permute-start | bytes 5505032 | tf_op jit(solution)/shard_map/ppermute | solution.py:292
  18.7 14.4 %collective-permute-start.3 = (bf16[2,1792]{1,0:T(2,128)(2,1)S(1)}, bf16[2,1792]{1,0:T(2,128)(2,1)S(1)}, u32[]{:S(2)}, u32[]{:S(2)}) collective-permute-start(bf16[2,1792]{1,0:T(2,128)(2,1)S(1)} %dynamic-slice_bitcast_fusion.2), channel_id=1, source_target_pairs={{0,1},{1,0},{2,3},{3,2},{4,5},{5,4},{6,7},{7,6},{8,9},{9,8},{10,11... | collective-permute-start | bytes 21512 | tf_op jit(solution)/shard_map/ppermute | solution.py:295
  27.3 5.3 %copy-start.5 = (f32[1,128]{1,0:T(1,128)S(1)}, f32[1,128]{1,0:T(1,128)}, u32[]{:S(2)}) copy-start(f32[1,128]{1,0:T(1,128)} %param.9) | copy-start | bytes 1540
  27.4 5.0 %collective-permute-start = (bf16[64,3584]{1,0:T(8,128)(2,1)S(1)}, bf16[64,3584]{1,0:T(8,128)(2,1)S(1)}, u32[]{:S(2)}, u32[]{:S(2)}) collective-permute-start(bf16[64,3584]{1,0:T(8,128)(2,1)S(1)} %bitcast.42), channel_id=1, source_target_pairs={{0,1},{1,0},{2,3},{3,2},{4,5},{5,4},{6,7},{7,6},{8,9},{9,8},{10,11... | collective-permute-start | bytes 1376264 | tf_op jit(solution)/shard_map/ppermute | solution.py:310
  32.7 1.3 %collective-permute-start.1 = (bf16[128,128]{1,0:T(8,128)(2,1)S(1)}, bf16[128,128]{1,0:T(8,128)(2,1)S(1)}, u32[]{:S(2)}, u32[]{:S(2)}) collective-permute-start(bf16[128,128]{1,0:T(8,128)(2,1)S(1)} %fusion.5.feats), channel_id=1, source_target_pairs={{0,1},{1,0},{2,3},{3,2},{4,5},{5,4},{6,7},{7,6},{8,9},{9,8},{10,11... | collective-permute-start | bytes 98312 | tf_op jit(solution)/shard_map/ppermute | solution.py:315
  88.9 30.1 %copy-start.1 = (bf16[1,4,128,3584]{3,2,1,0:T(8,128)(2,1)S(1)}, bf16[1,4,128,3584]{3,2,1,0:T(8,128)(2,1)}, u32[]{:S(2)}) copy-start(bf16[1,4,128,3584]{3,2,1,0:T(8,128)(2,1)} %param.11) | copy-start | bytes 11010052
  114.6 7.9 %collective-permute-start.4 = (bf16[4,16,2,8,896]{4,3,2,1,0:T(8,128)(2,1)S(1)}, bf16[4,16,2,8,896]{4,3,2,1,0:T(8,128)(2,1)S(1)}, u32[]{:S(2)}, u32[]{:S(2)}) collective-permute-start(bf16[4,16,2,8,896]{4,3,2,1,0:T(8,128)(2,1)S(1)} %bitcast.39), channel_id=1, source_target_pairs={{0,1},{1,0},{2,3},{3,2},{4,5},{5,4},{6,7},{7,6},{8,9},{9,8},{10,11... | collective-permute-start | bytes 5505032 | tf_op jit(solution)/shard_map/ppermute | solution.py:326

commit v7 on v6

--- a/solution.py
+++ b/solution.py
@@ -35,7 +35,10 @@
     return copies
 
 
-def copies_kernel(acts, out):
+def copies_kernel(source, out, acts, sem):
+    load = pltpu.make_async_copy(source, acts, sem)
+    load.start()
+    load.wait()
     tiles = [acts[0, :, start : start + 128].astype(F32) for start in range(0, acts.shape[2], 128)]
     packed = jnp.concatenate(tiles, axis=0).astype(BF16)
     out[...] = jnp.broadcast_to(packed[None], out.shape)
@@ -45,8 +48,9 @@
     _, held, width = acts.shape
     return pl.pallas_call(
         copies_kernel,
-        in_specs=[VMEM],
+        in_specs=[ANY],
         out_specs=VMEM,
+        scratch_shapes=[pltpu.VMEM(acts.shape, BF16), pltpu.SemaphoreType.DMA],
         out_shape=jax.ShapeDtypeStruct((chips, held * width // 128, 128), BF16),
         compiler_params=params(4),
         cost_estimate=cost(0, 2 * chips * held * width),

time: 128 us -> 128 us (level)
  no operation moved by 1% of the time
where the time goes in v7:
time: 128 us; the launch traced here: 127 us
  blocking collectives  77 us (60%)
  starting transfers between devices  21.4 us (17%)
  Pallas kernels  12.1 us (9%)
  waiting for transfers between devices  9.25 us (7%)
  local copies, waits for them, and re-layouts  5.85 us (5%)
    all_to_all x1, blocking collectives, per_device(): lax.all_to_all(partials.reshape(16, rows // 4, half), ('y', 'x'), 0, 0, t...  30.1 us
    all_to_all x1, blocking collectives, per_device(): lax.all_to_all(jnp.broadcast_to(near[None], (16,) + near.shape), ('y', 'x...  25.6 us
    all_to_all x1, starting transfers between devices, per_device(): same = lax.all_to_all(copies, ('x', 'z'), 0, 0, tiled=True)  11.9 us
    all_to_all x1, blocking collectives, per_device(): chunks = lax.all_to_all(add_pieces(pieces), 'z', 0, 0, tiled=True)  11.1 us
    all_to_all x1, blocking collectives, per_device(): lax.all_to_all(jnp.broadcast_to(err[None], chunks.shape), 'z', 0, 0, tile...  10.2 us
    all_to_all x1, waiting for transfers between devices, per_device(): same = lax.all_to_all(copies, ('x', 'z'), 0, 0, tiled=True)  7.28 us
    pallas_call x1, Pallas kernels, other_half(): pl.pallas_call(other_half_kernel, in_specs=[SMEM, VMEM, VMEM, VMEM, VMEM,...  4.68 us
    ppermute x1, starting transfers between devices, per_device(): errs_other = lax.ppermute(errs, 'c', SWAP)  4.47 us
  transfers between devices with their start and end apart: 6, of which 4 were waited for; matrix products, arithmetic and copies ran while one was open for 4% of the time, Pallas kernels for 3%

profile of v7, /device:TPU:1, one launch (start us, length us, event | category | flops | bytes accessed | tf_op | source)
XLA Modules:
  0.0 127.2 jit_solution(2110144217017026052)
XLA Ops:
  0.6 0.0 copy-start
  0.6 0.0 copy-start.2
  0.7 0.8 copy-done.2
  1.4 0.8 copies_of_rows.1
  2.3 11.9 %all-to-all-start = ((bf16[32,56,128]{2,1,0:T(8,128)(2,1)}), bf16[32,56,128]{2,1,0:T(8,128)(2,1)S(1)}, u32[]{:S(2)}, u32[]{:S(2)}) async-start(bf16[32,56,128]{2,1,0:T(8,128)(2,1)} %copies_of_rows.1), calls=%async_computation | async-start | bytes 917504 | tf_op jit(solution)/shard_map/all_to_all | solution.py:291
  14.2 0.0 copy-start.4
  14.2 0.0 copy-start.3
  14.2 3.6 %dynamic-slice_bitcast_fusion = (bf16[4,128,1792]{2,1,0:T(8,128)(2,1)}, bf16[4,128,1792]{2,1,0:T(8,128)(2,1)S(1)}) fusion(bf16[1,4,128,3584]{3,2,1,0:T(8,128)(2,1)} %param.11, s32[]{:T(128)S(6)} %select_n.40, s32[]{:T(128)S(6)} %select_n.34), kind=kLoop, calls=%fused_computation | loop fusion | bytes 7340040 | tf_op jit(solution)/shard_map/dynamic_slice | solution.py:294
  17.8 1.0 collective-permute-start.2
  18.7 0.0 copy-done.4
  18.7 0.1 collective-permute-start.3
  18.8 0.8 dynamic-slice_reduce_fusion
  19.7 0.1 pad_add_fusion.1.layer.places
  19.7 0.0 copy-done.3
  19.8 7.3 %all-to-all-done = bf16[32,56,128]{2,1,0:T(8,128)(2,1)S(1)} async-done(((bf16[32,56,128]{2,1,0:T(8,128)(2,1)}), bf16[32,56,128]{2,1,0:T(8,128)(2,1)S(1)}, u32[]{:S(2)}, u32[]{:S(2)}) %all-to-all-start) | async-done | bytes 458784 | tf_op jit(solution)/shard_map/all_to_all | solution.py:291
  27.1 0.1 copy.15
  27.2 0.2 copy.22
  27.4 0.0 copy-start.5
  27.4 3.5 %collective-permute-start = (bf16[64,3584]{1,0:T(8,128)(2,1)S(1)}, bf16[64,3584]{1,0:T(8,128)(2,1)S(1)}, u32[]{:S(2)}, u32[]{:S(2)}) collective-permute-start(bf16[64,3584]{1,0:T(8,128)(2,1)S(1)} %bitcast.42), channel_id=1, source_target_pairs={{0,1},{1,0},{2,3},{3,2},{4,5},{5,4},{6,7},{7,6},{8,9},{9,8},{10,11... | collective-permute-start | bytes 1376264 | tf_op jit(solution)/shard_map/ppermute | solution.py:314
  31.0 0.0 copy-done
  31.0 0.3 fusion.2
  31.3 1.1 collective-permute-done.apart
  32.4 0.3 fusion
  32.7 0.0 copy-done.5
  32.7 0.5 collective-permute-start.1
  33.2 0.0 collective-permute-done.3
  33.2 0.8 collective-permute-done.1.feats_other
  34.0 0.0 collective-permute-done.2.got
  34.0 2.8 %recon_partials.1 = bf16[4,128,1792]{2,1,0:T(8,128)(2,1)S(1)} custom-call(s32[2]{0:T(128)S(1)} %pad_add_fusion.1.layer.places, bf16[128,128]{1,0:T(8,128)(2,1)S(1)} %fusion.5.feats, bf16[128,128]{1,0:T(8,128)(2,1)S(1)} %collective-permute-done.1.feats_other, bf16[4,128,1792]{2,1,0:T(8,128)(2,1)S(1)} %get-tuple-element.17.mine, ...), custom_call_target="tpu_custom_call" | custom-call | flops 469762048 | bytes 5505024 | tf_op jit(solution)/shard_map/recon_partials/pallas_call | solution.py:88
  36.9 30.1 %all_to_all.25.pieces = bf16[16,32,1792]{2,1,0:T(8,128)(2,1)S(1)} all-to-all(bf16[16,32,1792]{2,1,0:T(8,128)(2,1)S(1)} %bitcast.41), channel_id=1, replica_groups=mesh['y'=4,'x'=4,'z'=8,'c'=2] {'y','x'}, dimensions={0} | all-to-all | bytes 3670016 | tf_op jit(solution)/shard_map/all_to_all | solution.py:323
  66.9 0.4 add_pieces.1
  67.3 11.1 %all_to_all.26 = bf16[8,8,896]{2,1,0:T(8,128)(2,1)S(1)} all-to-all(bf16[8,8,896]{2,1,0:T(8,128)(2,1)S(1)} %add_pieces.1), channel_id=1, replica_groups=mesh['y'=4,'x'=4,'z'=8,'c'=2] {'z'}, dimensions={0} | all-to-all | bytes 229376 | tf_op jit(solution)/shard_map/all_to_all | solution.py:324
  78.5 10.2 %all_to_all.27 = bf16[8,8,896]{2,1,0:T(8,128)(2,1)S(1)} all-to-all(bf16[8,8,896]{2,1,0:T(8,128)(2,1)S(1)} %broadcast_in_dim.11), channel_id=1, replica_groups=mesh['y'=4,'x'=4,'z'=8,'c'=2] {'z'}, dimensions={0} | all-to-all | bytes 229376 | tf_op jit(solution)/shard_map/all_to_all | solution.py:327
  88.7 0.2 broadcast_in_dim.24
  89.0 0.0 copy-start.1
  89.0 25.6 %all_to_all.28 = bf16[16,8,8,896]{3,2,1,0:T(8,128)(2,1)S(1)} all-to-all(bf16[16,8,8,896]{3,2,1,0:T(8,128)(2,1)S(1)} %broadcast_in_dim.24), channel_id=1, replica_groups=mesh['y'=4,'x'=4,'z'=8,'c'=2] {'y','x'}, dimensions={0} | all-to-all | bytes 3670016 | tf_op jit(solution)/shard_map/all_to_all | solution.py:328
  114.6 4.5 %collective-permute-start.4 = (bf16[4,16,2,8,896]{4,3,2,1,0:T(8,128)(2,1)S(1)}, bf16[4,16,2,8,896]{4,3,2,1,0:T(8,128)(2,1)S(1)}, u32[]{:S(2)}, u32[]{:S(2)}) collective-permute-start(bf16[4,16,2,8,896]{4,3,2,1,0:T(8,128)(2,1)S(1)} %bitcast.39), channel_id=1, source_target_pairs={{0,1},{1,0},{2,3},{3,2},{4,5},{5,4},{6,7},{7,6},{8,9},{9,8},{10,11... | collective-permute-start | bytes 5505032 | tf_op jit(solution)/shard_map/ppermute | solution.py:330
  119.1 0.0 copy-done.1
  119.1 3.3 %own_half.1 = (bf16[4,128,3584]{2,1,0:T(8,128)(2,1)}, f32[128,128]{1,0:T(8,128)S(1)}, f32[1,1792]{1,0:T(1,128)S(1)}) custom-call(s32[2]{0:T(128)S(1)} %pad_add_fusion.1.layer.places, bf16[128,128]{1,0:T(8,128)(2,1)S(1)} %fusion.5.feats, bf16[4,16,2,8,896]{4,3,2,1,0:T(8,128)(2,1)S(1)} %bitcast.40, bf16[4,128,3584]{2,1,0:T(8,128)(2,1)S(1)} %bitcast.37), custom_call_target="tpu_custom_call" | custom-call | flops 469762048 | bytes 5505024 | tf_op jit(solution)/shard_map/own_half/pallas_call | solution.py:183
  122.4 0.1 collective-permute-done.4.errs
  122.5 4.7 %other_half.1 = (bf16[4,128,3584]{2,1,0:T(8,128)(2,1)}, f32[1,3584]{1,0:T(1,128)}, bf16[3584,128]{1,0:T(8,128)(2,1)}, f32[1,128]{1,0:T(1,128)}) custom-call(s32[2]{0:T(128)S(1)} %pad_add_fusion.1.layer.places, bf16[128,128]{1,0:T(8,128)(2,1)S(1)} %fusion.5.feats, s32[128,128]{1,0:T(8,128)S(1)} %pad_add_fusion.gate, ...), custom_call_target="tpu_custom_call", output_to_operand_aliasing={{0}: (9, {})} | custom-call | flops 704643072 | bytes 7340032 | tf_op jit(solution)/shard_map/other_half/pallas_call | solution.py:251
  (10 shorter events, 0.2 us)
Async XLA Ops:
  0.6 30.4 %copy-start = (bf16[1,3584,128]{2,1,0:T(8,128)(2,1)S(1)}, bf16[1,3584,128]{2,1,0:T(8,128)(2,1)}, u32[]{:S(2)}) copy-start(bf16[1,3584,128]{2,1,0:T(8,128)(2,1)} %param.8) | copy-start | bytes 2752516
  0.6 0.8 copy-start.2
  2.3 24.8 %all-to-all-start = ((bf16[32,56,128]{2,1,0:T(8,128)(2,1)}), bf16[32,56,128]{2,1,0:T(8,128)(2,1)S(1)}, u32[]{:S(2)}, u32[]{:S(2)}) async-start(bf16[32,56,128]{2,1,0:T(8,128)(2,1)} %copies_of_rows.1), calls=%async_computation | async-start | bytes 917504 | tf_op jit(solution)/shard_map/all_to_all | solution.py:291
  14.2 4.5 %copy-start.4 = (bf16[1,2,3584]{2,1,0:T(2,128)(2,1)S(1)}, bf16[1,2,3584]{2,1,0:T(2,128)(2,1)}, u32[]{:S(2)}) copy-start(bf16[1,2,3584]{2,1,0:T(2,128)(2,1)} %param.13) | copy-start | bytes 43012
  14.2 5.6 %copy-start.3 = (s32[1,128,128]{2,1,0:T(8,128)S(1)}, s32[1,128,128]{2,1,0:T(8,128)}, u32[]{:S(2)}) copy-start(s32[1,128,128]{2,1,0:T(8,128)} %param.10) | copy-start | bytes 196612
  17.8 16.3 %collective-permute-start.2 = (bf16[4,128,1792]{2,1,0:T(8,128)(2,1)}, bf16[4,128,1792]{2,1,0:T(8,128)(2,1)}, u32[]{:S(2)}, u32[]{:S(2)}) collective-permute-start(bf16[4,128,1792]{2,1,0:T(8,128)(2,1)} %get-tuple-element.26), channel_id=1, source_target_pairs={{0,1},{1,0},{2,3},{3,2},{4,5},{5,4},{6,7},{7,6},{8,9},{9,8},{10,11... | collective-permute-start | bytes 5505032 | tf_op jit(solution)/shard_map/ppermute | solution.py:296
  18.7 14.4 %collective-permute-start.3 = (bf16[2,1792]{1,0:T(2,128)(2,1)S(1)}, bf16[2,1792]{1,0:T(2,128)(2,1)S(1)}, u32[]{:S(2)}, u32[]{:S(2)}) collective-permute-start(bf16[2,1792]{1,0:T(2,128)(2,1)S(1)} %dynamic-slice_bitcast_fusion.2), channel_id=1, source_target_pairs={{0,1},{1,0},{2,3},{3,2},{4,5},{5,4},{6,7},{7,6},{8,9},{9,8},{10,11... | collective-permute-start | bytes 21512 | tf_op jit(solution)/shard_map/ppermute | solution.py:299
  27.4 5.3 %copy-start.5 = (f32[1,128]{1,0:T(1,128)S(1)}, f32[1,128]{1,0:T(1,128)}, u32[]{:S(2)}) copy-start(f32[1,128]{1,0:T(1,128)} %param.9) | copy-start | bytes 1540
  27.4 5.0 %collective-permute-start = (bf16[64,3584]{1,0:T(8,128)(2,1)S(1)}, bf16[64,3584]{1,0:T(8,128)(2,1)S(1)}, u32[]{:S(2)}, u32[]{:S(2)}) collective-permute-start(bf16[64,3584]{1,0:T(8,128)(2,1)S(1)} %bitcast.42), channel_id=1, source_target_pairs={{0,1},{1,0},{2,3},{3,2},{4,5},{5,4},{6,7},{7,6},{8,9},{9,8},{10,11... | collective-permute-start | bytes 1376264 | tf_op jit(solution)/shard_map/ppermute | solution.py:314
  32.7 1.3 %collective-permute-start.1 = (bf16[128,128]{1,0:T(8,128)(2,1)S(1)}, bf16[128,128]{1,0:T(8,128)(2,1)S(1)}, u32[]{:S(2)}, u32[]{:S(2)}) collective-permute-start(bf16[128,128]{1,0:T(8,128)(2,1)S(1)} %fusion.5.feats), channel_id=1, source_target_pairs={{0,1},{1,0},{2,3},{3,2},{4,5},{5,4},{6,7},{7,6},{8,9},{9,8},{10,11... | collective-permute-start | bytes 98312 | tf_op jit(solution)/shard_map/ppermute | solution.py:319
  89.0 30.1 %copy-start.1 = (bf16[1,4,128,3584]{3,2,1,0:T(8,128)(2,1)S(1)}, bf16[1,4,128,3584]{3,2,1,0:T(8,128)(2,1)}, u32[]{:S(2)}) copy-start(bf16[1,4,128,3584]{3,2,1,0:T(8,128)(2,1)} %param.11) | copy-start | bytes 11010052
  114.6 7.9 %collective-permute-start.4 = (bf16[4,16,2,8,896]{4,3,2,1,0:T(8,128)(2,1)S(1)}, bf16[4,16,2,8,896]{4,3,2,1,0:T(8,128)(2,1)S(1)}, u32[]{:S(2)}, u32[]{:S(2)}) collective-permute-start(bf16[4,16,2,8,896]{4,3,2,1,0:T(8,128)(2,1)S(1)} %bitcast.39), channel_id=1, source_target_pairs={{0,1},{1,0},{2,3},{3,2},{4,5},{5,4},{6,7},{7,6},{8,9},{9,8},{10,11... | collective-permute-start | bytes 5505032 | tf_op jit(solution)/shard_map/ppermute | solution.py:330
